TPU v7x, 32 devices: a whole 2x2x4 slice. The times are simulated.
32 devices in a mesh: groups: 2 (over y), leaf: 4 (over z), pair: 2 (over x), rhs: 2 (over core).
Axes of the slice: x: 2, y: 2, z: 4, core: 2. Of those that a mesh axis runs over, the one named last changes fastest.
Arguments:
- points: bfloat16 [128, 512, 64], P(('groups', 'leaf')), parts along dimension 0, may hold values from -6 to 6
- weights: bfloat16 [65536, 32], P(('groups', 'leaf'), 'rhs'), parts along dimension 0, may hold values from -6 to 6
- interp: bfloat16 [128, 256, 256], P(('groups', 'leaf')), parts along dimension 0, may hold values from -0.375 to 0.375
- tree_order: int32 [8, 8192], P(('groups', 'leaf')), parts along dimension 0, may hold values from 0 to 8191, each once within a row
- skel_order: int32 [128, 512], P(('groups', 'leaf')), parts along dimension 0, may hold values from 0 to 511, each once within a row
- near_pairs: int32 [128, 16], P(('groups', 'leaf'), 'pair'), parts along dimension 0, may hold values from 0 to 63, as said below
- far_pairs: int32 [128, 8], P(('groups', 'leaf'), 'pair'), parts along dimension 0, may hold values from 0 to 63, as said below
Outputs:
- product: float32 [65536, 32], P(('groups', 'leaf'), 'rhs'), parts along dimension 0
There are 2 independent parts, one for each index of `groups`. A program takes and returns all parts, laid end to end along the dimension named above; each array names one. Nothing has to cross between parts.
Inputs may be any that keep to these rules, and one draw needn't show every extreme that they name: `tree_order`: each row is a permutation of 0 to 8191. `skel_order`: each row is a permutation of 0 to 511; its first 256 entries are the skeleton points. `near_pairs`: every entry lies within 8 of its row's leaf; every row holds its own leaf and a leaf exactly 8 away. `far_pairs`: take the block of rows b * 16 to (b + 1) * 16 - 1 and columns p * 4 to (p + 1) * 4 - 1: its entries never lie in rows' own leaves b * 16 to (b + 1) * 16 - 1, and every block of leaves c * 16 to (c + 1) * 16 - 1 that its entries name is named by exactly 32 of them.
All inputs are finite; a program needn't handle non-finite values.
Results may differ from a plain program's by a relative error of at most 0.0035.
Values may be sent and summed in bfloat16 or wider, within the bound.
No kernel may reach another device: no remote copies, remote signals or barrier semaphores. Data moves between devices by JAX's collectives and lax.ppermute only.
A program may use at most 128 MiB of HBM per device.

v0:
```python
import functools

import jax
import jax.numpy as jnp
from jax import lax
from jax.experimental import pallas as pl
from jax.experimental.pallas import tpu as pltpu
from jax.sharding import PartitionSpec as P

BF = jnp.bfloat16
F32 = jnp.float32
LOG2E = 1.4426950408889634
EXTRA = 16
GROUP = 8
VMEM = pl.BlockSpec(memory_space=pltpu.VMEM)
SMEM = pl.BlockSpec(memory_space=pltpu.SMEM)


def call(body, shapes, specs, args, scratch=(), flops=0, out_specs=None, grant=48):
    outs = [jax.ShapeDtypeStruct(s, d) for s, d in shapes]
    return pl.pallas_call(
        body,
        out_shape=outs,
        in_specs=specs,
        out_specs=out_specs or [VMEM] * len(outs),
        scratch_shapes=list(scratch),
        compiler_params=pltpu.CompilerParams(vmem_limit_bytes=grant << 20),
        cost_estimate=pl.CostEstimate(flops=flops, bytes_accessed=1 << 20, transcendentals=0),
    )(*args)


def extra_rows(feat, ones_first):
    wide = feat.astype(F32)
    half = -0.5 * jnp.sum(wide * wide, axis=0, keepdims=True)
    high = half.astype(BF).astype(F32)
    mid = (half - high).astype(BF).astype(F32)
    low = half - high - mid
    row = lax.broadcasted_iota(jnp.int32, (EXTRA, feat.shape[1]), 0)
    at = 3 if ones_first else 0
    ones = (row < 3) if ones_first else (row >= 3) & (row < 6)
    picked = jnp.where(row == at, high, jnp.where(row == at + 1, mid, jnp.where(row == at + 2, low, 0.0)))
    return jnp.where(ones, 1.0, picked).astype(BF)


def as_targets(feat):
    return jnp.concatenate([feat, extra_rows(feat, False)], axis=0)


def as_sources(feat):
    return jnp.concatenate([feat, extra_rows(feat, True)], axis=0).astype(F32).T.astype(BF)


def one_hot(row_ids, count):
    rows = lax.broadcasted_iota(jnp.int32, (count, row_ids.shape[1]), 0)
    return jnp.where(rows == row_ids, 1.0, 0.0).astype(BF)


def dot(a, b):
    return jnp.dot(a, b, preferred_element_type=F32)


def dot_last(a, b):
    return lax.dot_general(a, b, (((1,), (1,)), ((), ())), preferred_element_type=F32)


def gauss(sources, targets, scale):
    return jnp.exp2(dot(sources, targets) * scale).astype(BF)


def class_of():
    return lax.axis_index("pair") * lax.axis_size("rhs") + lax.axis_index("rhs")


def halo_body(classes, pts_ref, near_ref, far_ref, up_ref, down_ref, pairs_ref, near_buf, far_buf, sems):
    halo = up_ref.shape[0]
    half = pts_ref.shape[0] // 2
    copies = [
        pltpu.make_async_copy(near_ref, near_buf, sems.at[2 * halo]),
        pltpu.make_async_copy(far_ref, far_buf, sems.at[2 * halo + 1]),
    ]
    for j in range(halo):
        leaf = class_of() + j * classes
        copies.append(pltpu.make_async_copy(pts_ref.at[leaf + half], up_ref.at[j], sems.at[j]))
        copies.append(pltpu.make_async_copy(pts_ref.at[leaf], down_ref.at[j], sems.at[halo + j]))
    for copy in copies:
        copy.start()
    for copy in copies:
        copy.wait()
    near_n = near_ref.shape[0]
    pairs_ref[:near_n] = near_buf[...]
    pairs_ref[near_n:] = far_buf[...]


def weights_body(
    blocks, classes, near_n, span, halo, own_ref, other_ref, order_ref, skel_ref, interp_ref, pts_ref, *refs
):
    pair_refs = refs[:-13]
    tw_ref, up_ref, mid_ref, down_ref, cnt_ref, far_ref = refs[-13:-7]
    stack, own_buf, order_buf, skel_buf, interp_buf, pts_buf, sems = refs[-7:]
    cols = own_ref.shape[0]
    step = 2 * cols
    width = stack.shape[1]
    turns = own_ref.shape[1] // width
    mine, _, size = tw_ref.shape
    rank = mid_ref.shape[1]
    dim = pts_ref.shape[1]
    cuts = size // rank
    leaves = pts_ref.shape[0]
    block, me = lax.axis_index("leaf"), class_of()
    base = block * leaves - span
    copies = [
        pltpu.make_async_copy(own_ref, own_buf, sems.at[0]),
        pltpu.make_async_copy(order_ref, order_buf, sems.at[1]),
        pltpu.make_async_copy(skel_ref, skel_buf, sems.at[2]),
    ]
    for j in range(mine):
        leaf = j * classes + me
        copies.append(pltpu.make_async_copy(interp_ref.at[leaf], interp_buf.at[j], sems.at[3 + 2 * j]))
        copies.append(pltpu.make_async_copy(pts_ref.at[leaf], pts_buf.at[j], sems.at[4 + 2 * j]))
    for copy in copies:
        copy.start()
    for e in range(cnt_ref.shape[0]):
        wanted = base + e * classes + me
        total = None
        for ref in pair_refs:
            part = jnp.sum(jnp.where(ref[:near_n] == wanted, 1, 0), axis=0, keepdims=True)
            total = part if total is None else total + part
        cnt_ref[e : e + 1] = total
    far_n = far_ref.shape[0] // len(pair_refs)
    for k, ref in enumerate(pair_refs):
        named = ref[near_n:]
        owner = lax.div(named, leaves)
        within = lax.rem(named, leaves)
        piece = lax.rem(block - owner + blocks, blocks) - 1
        target = lax.broadcasted_iota(jnp.int32, named.shape, 1)
        code = target * 256 + piece * mine + lax.div(within, classes)
        far_ref[k * far_n : (k + 1) * far_n] = jnp.where(lax.rem(within, classes) == me, code, -1)

    copies[0].wait()
    copies[1].wait()
    for hi in range(turns):
        span = slice(hi * width, (hi + 1) * width)
        stack[hi * step : hi * step + cols] = own_buf[:, span]
        stack[hi * step + cols : (hi + 1) * step] = other_ref[:, span]
    orders = {}
    for j in range(mine):
        leaf = j * classes + me
        ids = order_buf[:, pl.ds(pl.multiple_of(leaf * size, size), size)]
        hi_ids = lax.shift_right_logical(ids, width.bit_length() - 1)
        picked = dot(stack[...], one_hot(ids & (width - 1), width))
        total = jnp.zeros((step, size), F32)
        for hi in range(turns):
            total = total + jnp.where(hi_ids == hi, picked[hi * step : (hi + 1) * step], 0.0)
        tree = total.astype(BF)
        tw_ref[j] = tree
        if j == 0:
            for copy in copies[2:]:
                copy.wait()
        hot = one_hot(skel_buf[pl.ds(leaf, 1), :], size)
        ordered = dot(tree, hot)
        combined = dot_last(ordered[:, rank:].astype(BF), interp_buf[j])
        skel_p = dot(pts_buf[j], hot[:, :rank]).astype(BF)
        skel_w = (ordered[:, :rank] + combined).astype(BF)
        for ref, low, high in ((up_ref, 0, mine - halo), (mid_ref, 0, mine), (down_ref, halo, mine)):
            weights_at, halo_at = (high - low) * dim, (high - low) * dim + mine * step
            if low <= j < high:
                ref[(j - low) * dim : (j - low + 1) * dim] = skel_p
            elif ref is not mid_ref:
                place = j - (mine - halo) if low == 0 else j
                for cut in range(cuts):
                    at = halo_at + (place * cuts + cut) * step
                    ref[at : at + step] = tree[:, cut * rank : (cut + 1) * rank]
                row = lax.broadcasted_iota(jnp.int32, (EXTRA, rank), 0)
                picks = skel_buf[pl.ds(leaf, 1), :rank]
                high_half = jnp.where(row == 2 * place, lax.shift_right_logical(picks, 8), 0)
                halves = jnp.where(row == 2 * place + 1, picks & 255, high_half).astype(F32)
                before = orders.get(id(ref))
                orders[id(ref)] = halves if before is None else before + halves
                ref[halo_at + halo * cuts * step :] = orders[id(ref)].astype(BF)
            ref[weights_at + j * step : weights_at + (j + 1) * step] = skel_w


def list_named(t, first, count, cnt_ref, slots, at):
    found = jnp.int32(0)
    for e in range(count):
        slots[at + found] = jnp.int32(e)
        found = found + jnp.where(cnt_ref[first + e, t] > 0, 1, 0)
    return found


def named_sum(t, k, first, scale, cnt_ref, slots, at, tgt, src, weights, shift):
    if k == 0:
        return jnp.zeros((weights.shape[1], tgt.shape[2]), F32)
    names = [slots[at + j] for j in range(k)]
    size = src.shape[1]
    block = gauss(jnp.concatenate([src[s + shift] for s in names], axis=0), tgt[t], scale)
    total = None
    for j, s in enumerate(names):
        times = cnt_ref[first + s, t].astype(F32)
        part = dot(weights[s + shift], block[j * size : (j + 1) * size]) * times
        total = part if total is None else total + part
    return total


def near_body(
    halo, scale, cnt_ref, pts_ref, tw_ref, left_p, right_p, skel_ref,
    near_ref, tgt_ref, edge_src, far_tgt_ref, src, slots,
):
    leaves, _, size = pts_ref.shape
    mine = tw_ref.shape[0]
    classes = leaves // mine
    rank = far_tgt_ref.shape[2]

    def sources(j, _):
        src[j] = as_sources(pts_ref[j * classes + class_of()])
        return 0

    lax.fori_loop(0, mine, sources, 0)
    tgt_ref[0] = as_targets(pts_ref[0])

    def target(t, _):
        found = list_named(t, halo, mine, cnt_ref, slots, 0)
        for k in range(mine + 1):

            @pl.when(found == k)
            def _():
                total = named_sum(t, k, halo, scale, cnt_ref, slots, 0, tgt_ref, src, tw_ref, 0)
                hot = one_hot(skel_ref[pl.ds(t, 1), :rank], size)
                far_tgt = as_targets(dot(pts_ref[t], hot).astype(BF))
                later = jnp.minimum(t + 1, leaves - 1)
                following = as_targets(pts_ref[later])
                near_ref[t] = total
                far_tgt_ref[t] = far_tgt
                tgt_ref[later] = following

        return 0

    lax.fori_loop(0, leaves, target, 0)
    for j in range(halo):
        edge_src[j] = as_sources(left_p[j])
        edge_src[halo + j] = as_sources(right_p[j])


def edge_body(
    halo, mine, rank, scale, cnt_ref, near_ref, tgt_ref, src, left_m, right_m, own_ref, other_ref, wts, slots
):
    leaves, cols2, size = near_ref.shape
    cols = cols2 // 2
    quarter = leaves // 4
    cuts = size // rank
    for side, message in enumerate((left_m, right_m)):
        for j in range(halo):
            for cut in range(cuts):
                at = message.shape[0] - EXTRA - (halo * cuts - j * cuts - cut) * cols2
                wts[side * halo + j, :, cut * rank : (cut + 1) * rank] = message[at : at + cols2]

    def targets(i, _):
        right = lax.div(i, quarter)
        first = right * (halo + mine)
        pair = (right * quarter + i, right * quarter + i + quarter)
        founds = [list_named(t, first, halo, cnt_ref, slots, n * (halo + 1)) for n, t in enumerate(pair)]
        for k in range((halo + 1) ** 2):
            counts = divmod(k, halo + 1)

            @pl.when((founds[0] == counts[0]) & (founds[1] == counts[1]))
            def _():
                sums = [
                    named_sum(t, c, first, scale, cnt_ref, slots, n * (halo + 1), tgt_ref, src, wts, right * halo)
                    for n, (t, c) in enumerate(zip(pair, counts))
                ]
                totals = [near_ref[t] + part for t, part in zip(pair, sums)]
                for t, total in zip(pair, totals):
                    span = pl.ds(pl.multiple_of(t * size, size), size)
                    own_ref[:, span] = total[:cols]
                    other_ref[:, span] = total[cols:].astype(BF)

        return 0

    lax.fori_loop(0, 2 * quarter, targets, 0)


def sources_body(mine, left_p, right_p, *refs):
    pieces = refs[:-2]
    far_src, far_w = refs[-2:]
    halo, dim, size = left_p.shape
    _, cols2, rank = far_w.shape
    for k, piece in enumerate(pieces):
        low, high, points = 0, mine, None
        if k == 0:
            high, points = mine - halo, left_p
        elif k == len(pieces) - 1:
            low, points = halo, right_p
        weights_at = (high - low) * dim
        for j in range(mine):
            if low <= j < high:
                skel_p = piece[(j - low) * dim : (j - low + 1) * dim]
            else:
                place = j - (mine - halo) if k == 0 else j
                order = piece[piece.shape[0] - EXTRA :].astype(F32)
                picks = (order[2 * place : 2 * place + 1] * 256.0 + order[2 * place + 1 : 2 * place + 2]).astype(jnp.int32)
                skel_p = dot(points[place], one_hot(picks, size)).astype(BF)
            far_src[k * mine + j] = as_sources(skel_p)
            far_w[k * mine + j] = piece[weights_at + j * cols2 : weights_at + (j + 1) * cols2]


def sum_body(own_ref, back_ref, *refs):
    first_ref, last_ref = refs[-2:]
    half = first_ref.shape[1]
    for ref, span in ((first_ref, slice(0, half)), (last_ref, slice(half, 2 * half))):
        ref[...] = (own_ref[:, span] + back_ref[:, span].astype(F32)).astype(BF)


def far_body(scale, far_ref, far_src, far_w, far_tgt, after_ref, own_ref, other_ref, field, names):
    found = jnp.int32(0)
    for t in range(far_ref.shape[1]):
        for i in range(far_ref.shape[0]):
            code = far_ref[i, t]
            names[1 + found] = code
            found = found + jnp.where(code >= 0, 1, 0)
    names[0] = found
    for j in range(GROUP):
        names[1 + found + j] = jnp.int32(far_ref.shape[1] * 256)
    leaves, _, rank = far_tgt.shape
    cols = own_ref.shape[0]
    field[...] = jnp.zeros_like(field)

    def far_group(g, _):
        codes = [names[1 + g * GROUP + j] for j in range(GROUP)]
        targets = [lax.shift_right_logical(c, 8) for c in codes]
        blocks = [gauss(far_src[c & 255], far_tgt[t & (leaves - 1)], scale) for c, t in zip(codes, targets)]
        parts = [dot(far_w[c & 255], block) for c, block in zip(codes, blocks)]
        for t, part in zip(targets, parts):
            field[t] += part
        return 0

    lax.fori_loop(0, lax.div(names[0] + GROUP - 1, GROUP), far_group, 0)
    for t in range(leaves):
        own_ref[:, t * rank : (t + 1) * rank] = field[t, :cols]
        other_ref[:, t * rank : (t + 1) * rank] = field[t, cols:].astype(BF)


def scatter(ids, value, width, turns):
    hi_ids = lax.shift_right_logical(ids, width.bit_length() - 1)
    masked = [jnp.where(hi_ids == hi, value, 0.0).astype(BF) for hi in range(turns)]
    return dot_last(jnp.concatenate(masked, axis=0), one_hot(ids & (width - 1), width))


def place_near_body(order_ref, *refs):
    near, acc = refs[:-1], refs[-1]
    total = order_ref.shape[1]
    width = acc.shape[1]
    chunk = 1024
    for at in range(0, total, chunk):
        span = slice(at, at + chunk)
        value = sum(ref[:, span].astype(F32) for ref in near)
        part = scatter(order_ref[:, span], value, width, total // width)
        acc[...] = part if at == 0 else acc[...] + part


def comp_body(order_ref, skel_ref, comp_ref):
    leaves, size = skel_ref.shape
    for t in range(leaves):
        span = slice(t * size, (t + 1) * size)
        ids = order_ref[:, span]
        row = lax.broadcasted_iota(jnp.int32, (16, size), 0)
        halves = jnp.where(row == 0, lax.shift_right_logical(ids, 8), jnp.where(row == 1, ids & 255, 0))
        moved = dot(halves.astype(F32).astype(BF), one_hot(skel_ref[t : t + 1], size))
        comp_ref[:, span] = (moved[:1] * 256.0 + moved[1:2]).astype(jnp.int32)


def place_far(first, comp_ref, interp_ref, start_ref, far, acc, buf):
    cols = far[0].shape[0]
    width = acc.shape[1]
    turns = acc.shape[0] // cols
    _, rank, rest = interp_ref.shape
    size = rank + rest
    for t in range(far[0].shape[1] // rank):
        skel = sum(ref[:, t * rank : (t + 1) * rank].astype(F32) for ref in far).astype(BF)
        buf[:, t * size : t * size + rank] = skel.astype(F32)
        buf[:, t * size + rank : (t + 1) * size] = dot(skel, interp_ref[first + t])
    chunk = 1024
    for at in range(0, buf.shape[1], chunk):
        ids = comp_ref[:, first * size + at : first * size + at + chunk]
        part = scatter(ids, buf[:, at : at + chunk], width, turns)
        acc[...] = (start_ref if at == 0 else acc)[...] + part


def place_first_body(comp_ref, interp_ref, start_ref, *refs):
    place_far(0, comp_ref, interp_ref, start_ref, refs[:-2], refs[-2], refs[-1])


def place_last_body(comp_ref, interp_ref, start_ref, *refs):
    far, out_ref, acc, buf = refs[:-3], refs[-3], refs[-2], refs[-1]
    place_far(interp_ref.shape[0] // 2, comp_ref, interp_ref, start_ref, far, acc, buf)
    cols, total = out_ref.shape
    width = acc.shape[1]
    for hi in range(total // width):
        out_ref[:, hi * width : (hi + 1) * width] = acc[hi * cols : (hi + 1) * cols]


def pin(value):
    return pltpu.with_memory_space_constraint(value, pltpu.HBM)


def ring(count, by):
    return [(i, (i + by) % count) for i in range(count)]


def from_others(value, axis):
    count = lax.axis_size(axis)
    return [lax.ppermute(value, axis, ring(count, by)) for by in range(1, count)]


def over_pair(value, pair_n):
    if pair_n == 2:
        return [value] + from_others(value, "pair")
    return list(lax.all_gather(value, "pair"))


def on_device(points, weights, interp, tree_order, skel_order, near_pairs, far_pairs):
    leaves, size, dim = points.shape
    rank = interp.shape[1]
    cols = weights.shape[1]
    blocks, pair_n, rhs_n = (lax.axis_size(a) for a in ("leaf", "pair", "rhs"))
    classes = pair_n * rhs_n
    mine = leaves // classes
    span = min(8, leaves)
    halo = span // classes
    scale = 2.0 * 2.5 / dim * LOG2E
    near_n, far_n = near_pairs.shape[1], far_pairs.shape[1]
    wide = dim + EXTRA
    mega = 10 ** 9
    pts = points.transpose(0, 2, 1)
    wts = weights.T
    (other_wts,) = from_others(wts, "rhs")
    hbm = pl.BlockSpec(memory_space=pltpu.HBM)
    up_p, down_p, pairs = call(
        functools.partial(halo_body, classes),
        [((halo, dim, size), BF), ((halo, dim, size), BF), ((near_n + far_n, leaves), jnp.int32)],
        [hbm, hbm, hbm],
        (pin(pts), pin(near_pairs.T), pin(far_pairs.T)),
        [
            pltpu.VMEM((near_n, leaves), jnp.int32),
            pltpu.VMEM((far_n, leaves), jnp.int32),
            pltpu.SemaphoreType.DMA((2 * halo + 2,)),
        ],
        out_specs=[hbm, hbm, VMEM],
        grant=48,
    )
    every = [pairs] + from_others(pairs, "pair")
    left_p = lax.ppermute(up_p, "leaf", ring(blocks, 1))
    right_p = lax.ppermute(down_p, "leaf", ring(blocks, blocks - 1))
    tall = mine * (dim + 2 * cols)
    ends = tall - halo * dim + halo * (size // rank) * 2 * cols + EXTRA
    tree_w, up_m, mid_m, down_m, cnt, far_ids = call(
        functools.partial(weights_body, blocks, classes, near_n, span, halo),
        [
            ((mine, 2 * cols, size), BF),
            ((ends, rank), BF),
            ((tall, rank), BF),
            ((ends, rank), BF),
            ((2 * halo + mine, leaves), jnp.int32),
            ((pair_n * far_n, leaves), jnp.int32),
        ],
        [hbm, VMEM] + [hbm] * 4 + [VMEM] * pair_n,
        (pin(wts), other_wts, pin(tree_order), pin(skel_order), pin(interp), pin(pts), *every),
        [
            pltpu.VMEM((2 * cols * (leaves * size // 256), 256), BF),
            pltpu.VMEM((cols, leaves * size), BF),
            pltpu.VMEM((1, leaves * size), jnp.int32),
            pltpu.VMEM((leaves, size), jnp.int32),
            pltpu.VMEM((mine, rank, size - rank), BF),
            pltpu.VMEM((mine, dim, size), BF),
            pltpu.SemaphoreType.DMA((3 + 2 * mine,)),
        ],
        flops=3 * mega,
        grant=48,
    )
    outgoing = {by: mid_m for by in range(1, blocks)} | {1: up_m, blocks - 1: down_m}
    pieces = [lax.ppermute(outgoing[by], "leaf", ring(blocks, by)) for by in range(1, blocks)]
    near, tgt, edge_src, far_tgt = call(
        functools.partial(near_body, halo, scale),
        [
            ((leaves, 2 * cols, size), F32),
            ((leaves, wide, size), BF),
            ((2 * halo, size, wide), BF),
            ((leaves, wide, rank), BF),
        ],
        [SMEM] + [VMEM] * 5,
        (cnt, pts, tree_w, left_p, right_p, skel_order),
        [pltpu.VMEM((mine, size, wide), BF), pltpu.SMEM((mine + 1,), jnp.int32)],
        flops=14 * mega,
    )

    near_own, near_other = call(
        functools.partial(edge_body, halo, mine, rank, scale),
        [((cols, leaves * size), F32), ((cols, leaves * size), BF)],
        [SMEM] + [VMEM] * 5,
        (cnt, near, tgt, edge_src, pieces[0], pieces[-1]),
        [pltpu.VMEM((2 * halo, 2 * cols, size), BF), pltpu.SMEM((2 * halo + 2,), jnp.int32)],
        flops=6 * mega,
    )
    (near_back,) = from_others(near_other, "rhs")
    near_sum_own = (near_own + near_back.astype(F32)).astype(BF)
    near_parts = over_pair(near_sum_own, pair_n)
    piece_n = (blocks - 1) * mine
    far_src, far_w = call(
        functools.partial(sources_body, mine),
        [((piece_n, rank, wide), BF), ((piece_n, 2 * cols, rank), BF)],
        [VMEM] * (blocks + 1),
        (left_p, right_p, *pieces),
        flops=2 * mega,
    )
    far_own, far_other = call(
        functools.partial(far_body, scale),
        [((cols, leaves * rank), F32), ((cols, leaves * rank), BF)],
        [SMEM, VMEM, VMEM, VMEM, pl.BlockSpec(memory_space=pl.ANY)],
        (far_ids, far_src, far_w, far_tgt, near_sum_own),
        [pltpu.VMEM((leaves + 1, 2 * cols, rank), F32), pltpu.SMEM((leaves * pair_n * far_n + 16,), jnp.int32)],
        flops=4 * mega,
    )
    (far_back,) = from_others(far_other, "rhs")
    (comp,) = call(
        comp_body, [((1, leaves * size), jnp.int32)], [VMEM] * 2, (tree_order, skel_order), flops=mega
    )
    halves = call(
        sum_body,
        [((cols, leaves // 2 * rank), BF)] * 2,
        [VMEM, VMEM] + [pl.BlockSpec(memory_space=pl.ANY)] * pair_n,
        (far_own, far_back, comp, *near_parts[1:]),
    )
    first_parts, last_parts = (over_pair(half, pair_n) for half in halves)
    acc_shape = (leaves * size // 256 * cols, 256)
    (acc,) = call(
        place_near_body,
        [(acc_shape, F32)],
        [VMEM] * (1 + pair_n),
        (tree_order, *near_parts),
        flops=3 * mega,
    )
    (acc,) = call(
        place_first_body,
        [(acc_shape, F32)],
        [VMEM] * (3 + pair_n),
        (comp, interp, acc, *first_parts),
        [pltpu.VMEM((cols, leaves // 2 * size), F32)],
        flops=2 * mega,
    )
    (out,) = call(
        place_last_body,
        [((cols, leaves * size), F32)],
        [VMEM] * (3 + pair_n),
        (comp, interp, acc, *last_parts),
        [pltpu.VMEM(acc_shape, F32), pltpu.VMEM((cols, leaves // 2 * size), F32)],
        flops=2 * mega,
    )
    return out.T


def solution(mesh):
    return jax.shard_map(
        on_device,
        mesh=mesh,
        in_specs=(
            P(("groups", "leaf"), None, None),
            P(("groups", "leaf"), "rhs"),
            P(("groups", "leaf"), None, None),
            P(("groups", "leaf"), None),
            P(("groups", "leaf"), None),
            P(("groups", "leaf"), "pair"),
            P(("groups", "leaf"), "pair"),
        ),
        out_specs=P(("groups", "leaf"), "rhs"),
        check_vma=False,
    )
```

profile of v0, /device:TPU:16, one launch (start us, length us, event | category | flops | bytes accessed | tf_op | source)
XLA Modules:
  0.0 51.0 jit_solution(8853504334653710931)
XLA Ops:
  0.0 1.0 %shard_map.74 = (bf16[2,64,512]{2,1,0:T(8,128)(2,1)S(1)}, bf16[2,64,512]{2,1,0:T(8,128)(2,1)S(1)}, s32[12,16]{1,0:T(8,128)S(1)}) custom-call(bf16[16,64,512]{2,1,0:T(8,128)(2,1)} %bitcast.5, s32[8,16]{1,0:T(8,128)} %bitcast.8, s32[4,16]{1,0:T(4,128)} %bitcast.9), custom_call_target="tpu_custom_call" | custom-call | bytes 1048576 | tf_op jit(solution)/shard_map/pallas_call | solution.py:21
  1.0 1.6 %collective-permute-start.1 = (s32[12,16]{1,0:T(8,128)S(1)}, s32[12,16]{1,0:T(8,128)S(1)}, u32[]{:S(2)}, u32[]{:S(2)}) collective-permute-start(s32[12,16]{1,0:T(8,128)S(1)} %get-tuple-element.26.refs_0_), channel_id=1, source_target_pairs={{0,2},{2,0},{1,3},{3,1},{4,6},{6,4},{5,7},{7,5},{8,10},{10,8},{9,1... | collective-permute-start | bytes 2312 | tf_op jit(solution)/shard_map/ppermute | solution.py:411
  2.6 1.6 %collective-permute-start.2 = (bf16[2,64,512]{2,1,0:T(8,128)(2,1)S(1)}, bf16[2,64,512]{2,1,0:T(8,128)(2,1)S(1)}, u32[]{:S(2)}, u32[]{:S(2)}) collective-permute-start(bf16[2,64,512]{2,1,0:T(8,128)(2,1)S(1)} %get-tuple-element.29), channel_id=1, source_target_pairs={{0,4},{4,8},{8,12},{12,0},{1,5},{5,9},{9,13},{13,1},{2,6},{6,10},{... | collective-permute-start | bytes 393224 | tf_op jit(solution)/shard_map/ppermute | solution.py:451
  4.2 0.4 collective-permute-start.3
  4.6 0.1 collective-permute-done.1.refs_1_
  4.7 3.7 %shard_map.75 = (bf16[4,32,512]{2,1,0:T(8,128)(2,1)S(1)}, bf16[400,256]{1,0:T(8,128)(2,1)S(1)}, bf16[384,256]{1,0:T(8,128)(2,1)S(1)}, bf16[400,256]{1,0:T(8,128)...) custom-call(bf16[16,8192]{1,0:T(8,128)(2,1)} %bitcast.11, bf16[16,8192]{1,0:T(8,128)(2,1)S(1)} %collective-permute-done.other_ref, ...), custom_call_target="tpu_custom_call" | custom-call | flops 3000000000 | bytes 1048576 | tf_op jit(solution)/shard_map/pallas_call | solution.py:21
  8.5 1.6 %collective-permute-start.4 = (bf16[400,256]{1,0:T(8,128)(2,1)S(1)}, bf16[400,256]{1,0:T(8,128)(2,1)S(1)}, u32[]{:S(2)}, u32[]{:S(2)}) collective-permute-start(bf16[400,256]{1,0:T(8,128)(2,1)S(1)} %get-tuple-element.34), channel_id=1, source_target_pairs={{0,4},{4,8},{8,12},{12,0},{1,5},{5,9},{9,13},{13,1},{2,6},{6,10},{... | collective-permute-start | bytes 614408 | tf_op jit(solution)/shard_map/ppermute | solution.py:480
  10.1 0.5 collective-permute-start.5
  10.5 3.8 %collective-permute-start.8 = (bf16[384,256]{1,0:T(8,128)(2,1)S(1)}, bf16[384,256]{1,0:T(8,128)(2,1)S(1)}, u32[]{:S(2)}, u32[]{:S(2)}) collective-permute-start(bf16[384,256]{1,0:T(8,128)(2,1)S(1)} %get-tuple-element.39), channel_id=1, source_target_pairs={{0,8},{4,12},{8,0},{12,4},{1,9},{5,13},{9,1},{13,5},{2,10},{6,14},... | collective-permute-start | bytes 589832 | tf_op jit(solution)/shard_map/ppermute | solution.py:480
  14.4 13.8 %shard_map.76 = (f32[16,32,512]{2,1,0:T(8,128)S(1)}, bf16[16,80,512]{2,1,0:T(8,128)(2,1)S(1)}, bf16[4,512,80]{2,1,0:T(8,128)(2,1)S(1)}, bf16[16,80,256]{2,1,0:T(8,128)(2,1)S(1)}) custom-call(s32[8,16]{1,0:T(8,128)S(1)} %get-tuple-element.27.cnt_ref, bf16[16,64,512]{2,1,0:T(8,128)(2,1)S(1)} %bitcast.7, bf16[4,32,512]{2,1,0:T(8,128)(2,1)S(1)} %get-tuple-element.28.tw_ref, ...), custom_call_target="tpu_custom_call" | custom-call | flops 14000000000 | bytes 1048576 | tf_op jit(solution)/shard_map/pallas_call | solution.py:21
  28.2 4.6 %shard_map.77 = (f32[16,8192]{1,0:T(8,128)S(1)}, bf16[16,8192]{1,0:T(8,128)(2,1)S(1)}) custom-call(s32[8,16]{1,0:T(8,128)S(1)} %get-tuple-element.27.cnt_ref, f32[16,32,512]{2,1,0:T(8,128)S(1)} %get-tuple-element.31.near_ref, bf16[16,80,512]{2,1,0:T(8,128)(2,1)S(1)} %get-tuple-element.32.tgt_ref, bf16[4,512,80]{2,1,0:T(8,128)(2,1)S(1)} %get-tuple-element.33.src, ...), custom_call_target="tpu_custom_call" | custom-call | flops 6000000000 | bytes 1048576 | tf_op jit(solution)/shard_map/pallas_call | solution.py:21
  32.7 0.1 collective-permute-start.6
  32.8 0.5 %shard_map.79 = (bf16[12,256,80]{2,1,0:T(8,128)(2,1)S(1)}, bf16[12,32,256]{2,1,0:T(8,128)(2,1)S(1)}) custom-call(bf16[2,64,512]{2,1,0:T(8,128)(2,1)S(1)} %collective-permute-done.2.left_p, bf16[2,64,512]{2,1,0:T(8,128)(2,1)S(1)} %collective-permute-done.3.right_p, bf16[400,256]{1,0:T(8,128)(2,1)S(1)} %collective-permute-done.4.left_m.refs_0_, ...), custom_call_target="tpu_custom_call" | custom-call | flops 2000000000 | bytes 1048576 | tf_op jit(solution)/shard_map/pallas_call | solution.py:21
  33.4 1.0 %collective-permute-done.6 = bf16[16,8192]{1,0:T(8,128)(2,1)S(1)} collective-permute-done((bf16[16,8192]{1,0:T(8,128)(2,1)S(1)}, bf16[16,8192]{1,0:T(8,128)(2,1)S(1)}, u32[]{:S(2)}, u32[]{:S(2)}) %collective-permute-start.6) | collective-permute-done | bytes 262176 | tf_op jit(solution)/shard_map/ppermute | solution.py:411
  34.4 0.1 collective-permute-start.7
  34.5 3.4 %shard_map.80 = (f32[16,4096]{1,0:T(8,128)S(1)}, bf16[16,4096]{1,0:T(8,128)(2,1)S(1)}) custom-call(s32[8,16]{1,0:T(8,128)S(1)} %get-tuple-element.38.far_ref, bf16[12,256,80]{2,1,0:T(8,128)(2,1)S(1)} %get-tuple-element.40.far_src, bf16[12,32,256]{2,1,0:T(8,128)(2,1)S(1)} %get-tuple-element.41.far_w, bf16[16,80,256]{2,1,0:T(8,128)(2,1)S(1)} %get-tuple-element.42.far_tgt, ...), custom_call_target="tpu_custom_call" | custom-call | flops 4000000000 | bytes 1048576 | tf_op jit(solution)/shard_map/pallas_call | solution.py:21
  37.9 0.2 collective-permute-start.9
  38.1 1.2 %shard_map.73.refs_0_.comp_ref = s32[1,8192]{1,0:T(1,128)S(1)} custom-call(s32[1,8192]{1,0:T(1,128)S(1)} %copy-done.3, s32[16,512]{1,0:T(8,128)S(1)} %copy-done.2), custom_call_target="tpu_custom_call" | custom-call | flops 1000000000 | bytes 1048576 | tf_op jit(solution)/shard_map/pallas_call | solution.py:21
  39.4 3.5 %collective-permute-done.7.refs_1_ = bf16[16,8192]{1,0:T(8,128)(2,1)S(1)} collective-permute-done((bf16[16,8192]{1,0:T(8,128)(2,1)S(1)}, bf16[16,8192]{1,0:T(8,128)(2,1)S(1)}, u32[]{:S(2)}, u32[]{:S(2)}) %collective-permute-start.7) | collective-permute-done | bytes 262176 | tf_op jit(solution)/shard_map/ppermute | solution.py:411
  42.9 0.4 collective-permute-start.10
  43.2 1.7 %collective-permute-start.11 = (bf16[16,2048]{1,0:T(8,128)(2,1)S(1)}, bf16[16,2048]{1,0:T(8,128)(2,1)S(1)}, u32[]{:S(2)}, u32[]{:S(2)}) collective-permute-start(bf16[16,2048]{1,0:T(8,128)(2,1)S(1)} %get-tuple-element.46.refs_0_), channel_id=1, source_target_pairs={{0,2},{2,0},{1,3},{3,1},{4,6},{6,4},{5,7},{7,5},{8,10},{10,8},{9,1... | collective-permute-start | bytes 196616 | tf_op jit(solution)/shard_map/ppermute | solution.py:411
  44.9 2.4 %shard_map.78.start_ref = f32[512,256]{1,0:T(8,128)S(1)} custom-call(s32[1,8192]{1,0:T(1,128)S(1)} %copy-done.3, bf16[16,8192]{1,0:T(8,128)(2,1)S(1)} %add_convert_fusion.refs_0_.after_ref, bf16[16,8192]{1,0:T(8,128)(2,1)S(1)} %collective-permute-done.7.refs_1_), custom_call_target="tpu_custom_call" | custom-call | flops 3000000000 | bytes 1048576 | tf_op jit(solution)/shard_map/pallas_call | solution.py:21
  47.4 1.4 %shard_map.82.start_ref = f32[512,256]{1,0:T(8,128)S(1)} custom-call(s32[1,8192]{1,0:T(1,128)S(1)} %shard_map.73.refs_0_.comp_ref, bf16[16,256,256]{2,1,0:T(8,128)(2,1)S(1)} %copy-done.1, f32[512,256]{1,0:T(8,128)S(1)} %shard_map.78.start_ref, bf16[16,2048]{1,0:T(8,128)(2,1)S(1)} %get-tuple-element.45.refs_0_, ...), custom_call_target="tpu_custom_call" | custom-call | flops 2000000000 | bytes 1048576 | tf_op jit(solution)/shard_map/pallas_call | solution.py:21
  48.8 2.2 %shard_map.83 = f32[16,8192]{1,0:T(8,128)} custom-call(s32[1,8192]{1,0:T(1,128)S(1)} %shard_map.73.refs_0_.comp_ref, bf16[16,256,256]{2,1,0:T(8,128)(2,1)S(1)} %copy-done.1, f32[512,256]{1,0:T(8,128)S(1)} %shard_map.82.start_ref, bf16[16,2048]{1,0:T(8,128)(2,1)S(1)} %get-tuple-element.46.refs_0_, bf16[16,2048]{1,0:T(8,128)(2,1)S(1)} %collective-permute-done.11.refs_1_), custom_call_target="tpu_custom_call" | custom-call | flops 2000000000 | bytes 1048576 | tf_op jit(solution)/shard_map/pallas_call | solution.py:21
  (20 shorter events, 0.1 us)
Async XLA Ops:
  0.0 4.7 %collective-permute-start = (bf16[16,8192]{1,0:T(8,128)(2,1)}, bf16[16,8192]{1,0:T(8,128)(2,1)S(1)}, u32[]{:S(2)}, u32[]{:S(2)}) collective-permute-start(bf16[16,8192]{1,0:T(8,128)(2,1)} %bitcast.10), channel_id=1, source_target_pairs={{0,1},{1,0},{2,3},{3,2},{4,5},{5,4},{6,7},{7,6},{8,9},{9,8},{10,11... | collective-permute-start | bytes 786440 | tf_op jit(solution)/shard_map/ppermute | solution.py:411
  1.0 3.7 %collective-permute-start.1 = (s32[12,16]{1,0:T(8,128)S(1)}, s32[12,16]{1,0:T(8,128)S(1)}, u32[]{:S(2)}, u32[]{:S(2)}) collective-permute-start(s32[12,16]{1,0:T(8,128)S(1)} %get-tuple-element.26.refs_0_), channel_id=1, source_target_pairs={{0,2},{2,0},{1,3},{3,1},{4,6},{6,4},{5,7},{7,5},{8,10},{10,8},{9,1... | collective-permute-start | bytes 2312 | tf_op jit(solution)/shard_map/ppermute | solution.py:411
  2.6 11.8 %collective-permute-start.2 = (bf16[2,64,512]{2,1,0:T(8,128)(2,1)S(1)}, bf16[2,64,512]{2,1,0:T(8,128)(2,1)S(1)}, u32[]{:S(2)}, u32[]{:S(2)}) collective-permute-start(bf16[2,64,512]{2,1,0:T(8,128)(2,1)S(1)} %get-tuple-element.29), channel_id=1, source_target_pairs={{0,4},{4,8},{8,12},{12,0},{1,5},{5,9},{9,13},{13,1},{2,6},{6,10},{... | collective-permute-start | bytes 393224 | tf_op jit(solution)/shard_map/ppermute | solution.py:451
  4.2 10.2 %copy-start = (bf16[16,512,64]{1,2,0:T(8,128)(2,1)S(1)}, bf16[16,512,64]{1,2,0:T(8,128)(2,1)}, u32[]{:S(2)}) copy-start(bf16[16,512,64]{1,2,0:T(8,128)(2,1)} %param.7) | copy-start | bytes 3145732
  4.2 10.2 %copy-start.2 = (s32[16,512]{1,0:T(8,128)S(1)}, s32[16,512]{1,0:T(8,128)}, u32[]{:S(2)}) copy-start(s32[16,512]{1,0:T(8,128)} %skel_ref.5) | copy-start | bytes 98308
  4.2 10.2 %collective-permute-start.3 = (bf16[2,64,512]{2,1,0:T(8,128)(2,1)S(1)}, bf16[2,64,512]{2,1,0:T(8,128)(2,1)S(1)}, u32[]{:S(2)}, u32[]{:S(2)}) collective-permute-start(bf16[2,64,512]{2,1,0:T(8,128)(2,1)S(1)} %get-tuple-element.30), channel_id=1, source_target_pairs={{0,12},{4,0},{8,4},{12,8},{1,13},{5,1},{9,5},{13,9},{2,14},{6,2},{... | collective-permute-start | bytes 393224 | tf_op jit(solution)/shard_map/ppermute | solution.py:452
  8.5 19.7 %collective-permute-start.4 = (bf16[400,256]{1,0:T(8,128)(2,1)S(1)}, bf16[400,256]{1,0:T(8,128)(2,1)S(1)}, u32[]{:S(2)}, u32[]{:S(2)}) collective-permute-start(bf16[400,256]{1,0:T(8,128)(2,1)S(1)} %get-tuple-element.34), channel_id=1, source_target_pairs={{0,4},{4,8},{8,12},{12,0},{1,5},{5,9},{9,13},{13,1},{2,6},{6,10},{... | collective-permute-start | bytes 614408 | tf_op jit(solution)/shard_map/ppermute | solution.py:480
  10.1 18.1 %collective-permute-start.5 = (bf16[400,256]{1,0:T(8,128)(2,1)S(1)}, bf16[400,256]{1,0:T(8,128)(2,1)S(1)}, u32[]{:S(2)}, u32[]{:S(2)}) collective-permute-start(bf16[400,256]{1,0:T(8,128)(2,1)S(1)} %get-tuple-element.35), channel_id=1, source_target_pairs={{0,12},{4,0},{8,4},{12,8},{1,13},{5,1},{9,5},{13,9},{2,14},{6,2},{... | collective-permute-start | bytes 614408 | tf_op jit(solution)/shard_map/ppermute | solution.py:480
  10.5 22.3 %collective-permute-start.8 = (bf16[384,256]{1,0:T(8,128)(2,1)S(1)}, bf16[384,256]{1,0:T(8,128)(2,1)S(1)}, u32[]{:S(2)}, u32[]{:S(2)}) collective-permute-start(bf16[384,256]{1,0:T(8,128)(2,1)S(1)} %get-tuple-element.39), channel_id=1, source_target_pairs={{0,8},{4,12},{8,0},{12,4},{1,9},{5,13},{9,1},{13,5},{2,10},{6,14},... | collective-permute-start | bytes 589832 | tf_op jit(solution)/shard_map/ppermute | solution.py:480
  32.7 1.6 %collective-permute-start.6 = (bf16[16,8192]{1,0:T(8,128)(2,1)S(1)}, bf16[16,8192]{1,0:T(8,128)(2,1)S(1)}, u32[]{:S(2)}, u32[]{:S(2)}) collective-permute-start(bf16[16,8192]{1,0:T(8,128)(2,1)S(1)} %get-tuple-element.37), channel_id=1, source_target_pairs={{0,1},{1,0},{2,3},{3,2},{4,5},{5,4},{6,7},{7,6},{8,9},{9,8},{10,11... | collective-permute-start | bytes 786440 | tf_op jit(solution)/shard_map/ppermute | solution.py:411
  34.4 8.4 %collective-permute-start.7 = (bf16[16,8192]{1,0:T(8,128)(2,1)S(1)}, bf16[16,8192]{1,0:T(8,128)(2,1)S(1)}, u32[]{:S(2)}, u32[]{:S(2)}) collective-permute-start(bf16[16,8192]{1,0:T(8,128)(2,1)S(1)} %add_convert_fusion.refs_0_.after_ref), channel_id=1, source_target_pairs={{0,2},{2,0},{1,3},{3,1},{4,6},{6,4},{5,7},{7,5},{8,10},{10,8},{9,1... | collective-permute-start | bytes 786440 | tf_op jit(solution)/shard_map/ppermute | solution.py:411
  34.5 3.6 %copy-start.3 = (s32[1,8192]{1,0:T(1,128)S(1)}, s32[1,8192]{1,0:T(1,128)}, u32[]{:S(2)}) copy-start(s32[1,8192]{1,0:T(1,128)} %order_ref.5) | copy-start | bytes 98308
  37.9 1.4 %collective-permute-start.9 = (bf16[16,4096]{1,0:T(8,128)(2,1)S(1)}, bf16[16,4096]{1,0:T(8,128)(2,1)S(1)}, u32[]{:S(2)}, u32[]{:S(2)}) collective-permute-start(bf16[16,4096]{1,0:T(8,128)(2,1)S(1)} %get-tuple-element.44), channel_id=1, source_target_pairs={{0,1},{1,0},{2,3},{3,2},{4,5},{5,4},{6,7},{7,6},{8,9},{9,8},{10,11... | collective-permute-start | bytes 393224 | tf_op jit(solution)/shard_map/ppermute | solution.py:411
  42.9 4.5 %collective-permute-start.10 = (bf16[16,2048]{1,0:T(8,128)(2,1)S(1)}, bf16[16,2048]{1,0:T(8,128)(2,1)S(1)}, u32[]{:S(2)}, u32[]{:S(2)}) collective-permute-start(bf16[16,2048]{1,0:T(8,128)(2,1)S(1)} %get-tuple-element.45.refs_0_), channel_id=1, source_target_pairs={{0,2},{2,0},{1,3},{3,1},{4,6},{6,4},{5,7},{7,5},{8,10},{10,8},{9,1... | collective-permute-start | bytes 196616 | tf_op jit(solution)/shard_map/ppermute | solution.py:411
  43.2 4.1 %copy-start.1 = (bf16[16,256,256]{2,1,0:T(8,128)(2,1)S(1)}, bf16[16,256,256]{2,1,0:T(8,128)(2,1)}, u32[]{:S(2)}) copy-start(bf16[16,256,256]{2,1,0:T(8,128)(2,1)} %interp_ref.5) | copy-start | bytes 6291460
  43.2 5.6 %collective-permute-start.11 = (bf16[16,2048]{1,0:T(8,128)(2,1)S(1)}, bf16[16,2048]{1,0:T(8,128)(2,1)S(1)}, u32[]{:S(2)}, u32[]{:S(2)}) collective-permute-start(bf16[16,2048]{1,0:T(8,128)(2,1)S(1)} %get-tuple-element.46.refs_0_), channel_id=1, source_target_pairs={{0,2},{2,0},{1,3},{3,1},{4,6},{6,4},{5,7},{7,5},{8,10},{10,8},{9,1... | collective-permute-start | bytes 196616 | tf_op jit(solution)/shard_map/ppermute | solution.py:411
where the time goes:
time: 50.8 us; the launch traced here: 51 us
  Pallas kernels  34.3 us (68%)
  starting transfers between devices  11.9 us (23%)
  waiting for transfers between devices  4.57 us (9%)
    pallas_call x11, Pallas kernels, call(): pl.pallas_call(body, out_shape=outs, in_specs=specs, out_specs=out_specs...  34.3 us
    ppermute x3, starting transfers between devices, on_device(): lax.ppermute(outgoing[by], 'leaf', ring(blocks, by))  5.88 us
    ppermute x7, waiting for transfers between devices, from_others(): lax.ppermute(value, axis, ring(count, by))  4.56 us
    ppermute x7, starting transfers between devices, from_others(): lax.ppermute(value, axis, ring(count, by))  3.99 us
    ppermute x1, starting transfers between devices, on_device(): left_p = lax.ppermute(up_p, 'leaf', ring(blocks, 1))  1.58 us
  transfers between devices with their start and end apart: 12, of which 3 were waited for; matrix products, arithmetic and copies ran while one was open for 0% of the time, Pallas kernels for 63%

commit v1 on v0

--- a/solution.py
+++ b/solution.py
@@ -94,9 +94,9 @@
 def weights_body(
     blocks, classes, near_n, span, halo, own_ref, other_ref, order_ref, skel_ref, interp_ref, pts_ref, *refs
 ):
-    pair_refs = refs[:-13]
-    tw_ref, up_ref, mid_ref, down_ref, cnt_ref, far_ref = refs[-13:-7]
-    stack, own_buf, order_buf, skel_buf, interp_buf, pts_buf, sems = refs[-7:]
+    pair_refs = refs[:-14]
+    tw_ref, up_ref, mid_ref, down_ref, cnt_ref, far_ref = refs[-14:-8]
+    stack, own_buf, order_buf, skel_buf, interp_buf, pts_buf, hots, sems = refs[-8:]
     cols = own_ref.shape[0]
     step = 2 * cols
     width = stack.shape[1]
@@ -151,16 +151,19 @@
         total = jnp.zeros((step, size), F32)
         for hi in range(turns):
             total = total + jnp.where(hi_ids == hi, picked[hi * step : (hi + 1) * step], 0.0)
-        tree = total.astype(BF)
-        tw_ref[j] = tree
-        if j == 0:
-            for copy in copies[2:]:
-                copy.wait()
-        hot = one_hot(skel_buf[pl.ds(leaf, 1), :], size)
-        ordered = dot(tree, hot)
-        combined = dot_last(ordered[:, rank:].astype(BF), interp_buf[j])
-        skel_p = dot(pts_buf[j], hot[:, :rank]).astype(BF)
-        skel_w = (ordered[:, :rank] + combined).astype(BF)
+        tw_ref[j] = total.astype(BF)
+    for copy in copies[2:]:
+        copy.wait()
+    for j in range(mine):
+        hots[j] = one_hot(skel_buf[pl.ds(j * classes + me, 1), :], size)
+    skel_ps = [dot(pts_buf[j], hots[j, :, :rank]).astype(BF) for j in range(mine)]
+    ordereds = [dot(tw_ref[j], hots[j]) for j in range(mine)]
+    combineds = [dot_last(ordereds[j][:, rank:].astype(BF), interp_buf[j]) for j in range(mine)]
+    for j in range(mine):
+        leaf = j * classes + me
+        tree = tw_ref[j]
+        skel_p = skel_ps[j]
+        skel_w = (ordereds[j][:, :rank] + combineds[j]).astype(BF)
         for ref, low, high in ((up_ref, 0, mine - halo), (mid_ref, 0, mine), (down_ref, halo, mine)):
             weights_at, halo_at = (high - low) * dim, (high - low) * dim + mine * step
             if low <= j < high:
@@ -471,6 +474,7 @@
             pltpu.VMEM((leaves, size), jnp.int32),
             pltpu.VMEM((mine, rank, size - rank), BF),
             pltpu.VMEM((mine, dim, size), BF),
+            pltpu.VMEM((mine, size, size), BF),
             pltpu.SemaphoreType.DMA((3 + 2 * mine,)),
         ],
         flops=3 * mega,

time: 50.8 us -> 50.3 us (level)
  the two profiles are of different devices: /device:TPU:16 before, /device:TPU:8 now
where the time goes in v1:
time: 50.3 us; the launch traced here: 50.1 us
  Pallas kernels  33.6 us (67%)
  starting transfers between devices  10.6 us (21%)
  waiting for transfers between devices  5.74 us (11%)
    pallas_call x11, Pallas kernels, call(): pl.pallas_call(body, out_shape=outs, in_specs=specs, out_specs=out_specs...  33.6 us
    ppermute x3, starting transfers between devices, on_device(): lax.ppermute(outgoing[by], 'leaf', ring(blocks, by))  4.67 us
    ppermute x7, waiting for transfers between devices, from_others(): lax.ppermute(value, axis, ring(count, by))  4.11 us
    ppermute x7, starting transfers between devices, from_others(): lax.ppermute(value, axis, ring(count, by))  3.86 us
    ppermute x3, waiting for transfers between devices, on_device(): lax.ppermute(outgoing[by], 'leaf', ring(blocks, by))  1.62 us
    ppermute x1, starting transfers between devices, on_device(): left_p = lax.ppermute(up_p, 'leaf', ring(blocks, 1))  1.58 us
  transfers between devices with their start and end apart: 12, of which 5 were waited for; matrix products, arithmetic and copies ran while one was open for 0% of the time, Pallas kernels for 62%

profile of v1, /device:TPU:8, one launch (start us, length us, event | category | flops | bytes accessed | tf_op | source)
XLA Modules:
  0.0 50.1 jit_solution(14915541202187031046)
XLA Ops:
  0.0 1.0 %shard_map.74 = (bf16[2,64,512]{2,1,0:T(8,128)(2,1)S(1)}, bf16[2,64,512]{2,1,0:T(8,128)(2,1)S(1)}, s32[12,16]{1,0:T(8,128)S(1)}) custom-call(bf16[16,64,512]{2,1,0:T(8,128)(2,1)} %bitcast.5, s32[8,16]{1,0:T(8,128)} %bitcast.8, s32[4,16]{1,0:T(4,128)} %bitcast.9), custom_call_target="tpu_custom_call" | custom-call | bytes 1048576 | tf_op jit(solution)/shard_map/pallas_call | solution.py:21
  1.0 1.6 %collective-permute-start.1 = (s32[12,16]{1,0:T(8,128)S(1)}, s32[12,16]{1,0:T(8,128)S(1)}, u32[]{:S(2)}, u32[]{:S(2)}) collective-permute-start(s32[12,16]{1,0:T(8,128)S(1)} %get-tuple-element.26.refs_0_), channel_id=1, source_target_pairs={{0,2},{2,0},{1,3},{3,1},{4,6},{6,4},{5,7},{7,5},{8,10},{10,8},{9,1... | collective-permute-start | bytes 2312 | tf_op jit(solution)/shard_map/ppermute | solution.py:414
  2.6 1.6 %collective-permute-start.2 = (bf16[2,64,512]{2,1,0:T(8,128)(2,1)S(1)}, bf16[2,64,512]{2,1,0:T(8,128)(2,1)S(1)}, u32[]{:S(2)}, u32[]{:S(2)}) collective-permute-start(bf16[2,64,512]{2,1,0:T(8,128)(2,1)S(1)} %get-tuple-element.29), channel_id=1, source_target_pairs={{0,4},{4,8},{8,12},{12,0},{1,5},{5,9},{9,13},{13,1},{2,6},{6,10},{... | collective-permute-start | bytes 393224 | tf_op jit(solution)/shard_map/ppermute | solution.py:454
  4.2 0.4 collective-permute-start.3
  4.6 0.1 collective-permute-done.1.refs_1_
  4.7 3.5 %shard_map.75 = (bf16[4,32,512]{2,1,0:T(8,128)(2,1)S(1)}, bf16[400,256]{1,0:T(8,128)(2,1)S(1)}, bf16[384,256]{1,0:T(8,128)(2,1)S(1)}, bf16[400,256]{1,0:T(8,128)...) custom-call(bf16[16,8192]{1,0:T(8,128)(2,1)} %bitcast.11, bf16[16,8192]{1,0:T(8,128)(2,1)S(1)} %collective-permute-done.other_ref, ...), custom_call_target="tpu_custom_call" | custom-call | flops 3000000000 | bytes 1048576 | tf_op jit(solution)/shard_map/pallas_call | solution.py:21
  8.2 1.6 %collective-permute-start.4 = (bf16[400,256]{1,0:T(8,128)(2,1)S(1)}, bf16[400,256]{1,0:T(8,128)(2,1)S(1)}, u32[]{:S(2)}, u32[]{:S(2)}) collective-permute-start(bf16[400,256]{1,0:T(8,128)(2,1)S(1)} %get-tuple-element.34), channel_id=1, source_target_pairs={{0,4},{4,8},{8,12},{12,0},{1,5},{5,9},{9,13},{13,1},{2,6},{6,10},{... | collective-permute-start | bytes 614408 | tf_op jit(solution)/shard_map/ppermute | solution.py:484
  9.9 0.6 %collective-permute-start.5 = (bf16[400,256]{1,0:T(8,128)(2,1)S(1)}, bf16[400,256]{1,0:T(8,128)(2,1)S(1)}, u32[]{:S(2)}, u32[]{:S(2)}) collective-permute-start(bf16[400,256]{1,0:T(8,128)(2,1)S(1)} %get-tuple-element.35), channel_id=1, source_target_pairs={{0,12},{4,0},{8,4},{12,8},{1,13},{5,1},{9,5},{13,9},{2,14},{6,2},{... | collective-permute-start | bytes 614408 | tf_op jit(solution)/shard_map/ppermute | solution.py:484
  10.5 2.4 %collective-permute-start.8 = (bf16[384,256]{1,0:T(8,128)(2,1)S(1)}, bf16[384,256]{1,0:T(8,128)(2,1)S(1)}, u32[]{:S(2)}, u32[]{:S(2)}) collective-permute-start(bf16[384,256]{1,0:T(8,128)(2,1)S(1)} %get-tuple-element.39), channel_id=1, source_target_pairs={{0,8},{4,12},{8,0},{12,4},{1,9},{5,13},{9,1},{13,5},{2,10},{6,14},... | collective-permute-start | bytes 589832 | tf_op jit(solution)/shard_map/ppermute | solution.py:484
  12.9 11.7 %shard_map.76 = (f32[16,32,512]{2,1,0:T(8,128)S(1)}, bf16[16,80,512]{2,1,0:T(8,128)(2,1)S(1)}, bf16[4,512,80]{2,1,0:T(8,128)(2,1)S(1)}, bf16[16,80,256]{2,1,0:T(8,128)(2,1)S(1)}) custom-call(s32[8,16]{1,0:T(8,128)S(1)} %get-tuple-element.27.cnt_ref, bf16[16,64,512]{2,1,0:T(8,128)(2,1)S(1)} %bitcast.7, bf16[4,32,512]{2,1,0:T(8,128)(2,1)S(1)} %get-tuple-element.28.tw_ref, ...), custom_call_target="tpu_custom_call" | custom-call | flops 14000000000 | bytes 1048576 | tf_op jit(solution)/shard_map/pallas_call | solution.py:21
  24.6 1.6 %collective-permute-done.5.right_m.refs_2_ = bf16[400,256]{1,0:T(8,128)(2,1)S(1)} collective-permute-done((bf16[400,256]{1,0:T(8,128)(2,1)S(1)}, bf16[400,256]{1,0:T(8,128)(2,1)S(1)}, u32[]{:S(2)}, u32[]{:S(2)}) %collective-permute-start.5) | collective-permute-done | bytes 204832 | tf_op jit(solution)/shard_map/ppermute | solution.py:484
  26.2 5.6 %shard_map.77 = (f32[16,8192]{1,0:T(8,128)S(1)}, bf16[16,8192]{1,0:T(8,128)(2,1)S(1)}) custom-call(s32[8,16]{1,0:T(8,128)S(1)} %get-tuple-element.27.cnt_ref, f32[16,32,512]{2,1,0:T(8,128)S(1)} %get-tuple-element.31.near_ref, bf16[16,80,512]{2,1,0:T(8,128)(2,1)S(1)} %get-tuple-element.32.tgt_ref, bf16[4,512,80]{2,1,0:T(8,128)(2,1)S(1)} %get-tuple-element.33.src, ...), custom_call_target="tpu_custom_call" | custom-call | flops 6000000000 | bytes 1048576 | tf_op jit(solution)/shard_map/pallas_call | solution.py:21
  31.8 0.1 collective-permute-start.6
  31.9 0.5 %shard_map.79 = (bf16[12,256,80]{2,1,0:T(8,128)(2,1)S(1)}, bf16[12,32,256]{2,1,0:T(8,128)(2,1)S(1)}) custom-call(bf16[2,64,512]{2,1,0:T(8,128)(2,1)S(1)} %collective-permute-done.2.left_p, bf16[2,64,512]{2,1,0:T(8,128)(2,1)S(1)} %collective-permute-done.3.right_p, bf16[400,256]{1,0:T(8,128)(2,1)S(1)} %collective-permute-done.4.left_m.refs_0_, ...), custom_call_target="tpu_custom_call" | custom-call | flops 2000000000 | bytes 1048576 | tf_op jit(solution)/shard_map/pallas_call | solution.py:21
  32.4 1.0 %collective-permute-done.6 = bf16[16,8192]{1,0:T(8,128)(2,1)S(1)} collective-permute-done((bf16[16,8192]{1,0:T(8,128)(2,1)S(1)}, bf16[16,8192]{1,0:T(8,128)(2,1)S(1)}, u32[]{:S(2)}, u32[]{:S(2)}) %collective-permute-start.6) | collective-permute-done | bytes 262176 | tf_op jit(solution)/shard_map/ppermute | solution.py:414
  33.6 4.0 %shard_map.80 = (f32[16,4096]{1,0:T(8,128)S(1)}, bf16[16,4096]{1,0:T(8,128)(2,1)S(1)}) custom-call(s32[8,16]{1,0:T(8,128)S(1)} %get-tuple-element.38.far_ref, bf16[12,256,80]{2,1,0:T(8,128)(2,1)S(1)} %get-tuple-element.40.far_src, bf16[12,32,256]{2,1,0:T(8,128)(2,1)S(1)} %get-tuple-element.41.far_w, bf16[16,80,256]{2,1,0:T(8,128)(2,1)S(1)} %get-tuple-element.42.far_tgt, ...), custom_call_target="tpu_custom_call" | custom-call | flops 4000000000 | bytes 1048576 | tf_op jit(solution)/shard_map/pallas_call | solution.py:21
  37.6 1.2 %shard_map.73.refs_0_.comp_ref = s32[1,8192]{1,0:T(1,128)S(1)} custom-call(s32[1,8192]{1,0:T(1,128)S(1)} %copy-done.3, s32[16,512]{1,0:T(8,128)S(1)} %copy-done.2), custom_call_target="tpu_custom_call" | custom-call | flops 1000000000 | bytes 1048576 | tf_op jit(solution)/shard_map/pallas_call | solution.py:21
  38.9 0.1 collective-permute-done.9.back_ref
  39.0 2.9 %collective-permute-done.7.refs_1_ = bf16[16,8192]{1,0:T(8,128)(2,1)S(1)} collective-permute-done((bf16[16,8192]{1,0:T(8,128)(2,1)S(1)}, bf16[16,8192]{1,0:T(8,128)(2,1)S(1)}, u32[]{:S(2)}, u32[]{:S(2)}) %collective-permute-start.7) | collective-permute-done | bytes 262176 | tf_op jit(solution)/shard_map/ppermute | solution.py:414
  41.9 0.4 collective-permute-start.10
  42.3 1.7 %collective-permute-start.11 = (bf16[16,2048]{1,0:T(8,128)(2,1)S(1)}, bf16[16,2048]{1,0:T(8,128)(2,1)S(1)}, u32[]{:S(2)}, u32[]{:S(2)}) collective-permute-start(bf16[16,2048]{1,0:T(8,128)(2,1)S(1)} %get-tuple-element.46.refs_0_), channel_id=1, source_target_pairs={{0,2},{2,0},{1,3},{3,1},{4,6},{6,4},{5,7},{7,5},{8,10},{10,8},{9,1... | collective-permute-start | bytes 196616 | tf_op jit(solution)/shard_map/ppermute | solution.py:414
  44.0 2.4 %shard_map.78.start_ref = f32[512,256]{1,0:T(8,128)S(1)} custom-call(s32[1,8192]{1,0:T(1,128)S(1)} %copy-done.3, bf16[16,8192]{1,0:T(8,128)(2,1)S(1)} %add_convert_fusion.refs_0_.after_ref, bf16[16,8192]{1,0:T(8,128)(2,1)S(1)} %collective-permute-done.7.refs_1_), custom_call_target="tpu_custom_call" | custom-call | flops 3000000000 | bytes 1048576 | tf_op jit(solution)/shard_map/pallas_call | solution.py:21
  46.4 1.4 %shard_map.82.start_ref = f32[512,256]{1,0:T(8,128)S(1)} custom-call(s32[1,8192]{1,0:T(1,128)S(1)} %shard_map.73.refs_0_.comp_ref, bf16[16,256,256]{2,1,0:T(8,128)(2,1)S(1)} %copy-done.1, f32[512,256]{1,0:T(8,128)S(1)} %shard_map.78.start_ref, bf16[16,2048]{1,0:T(8,128)(2,1)S(1)} %get-tuple-element.45.refs_0_, ...), custom_call_target="tpu_custom_call" | custom-call | flops 2000000000 | bytes 1048576 | tf_op jit(solution)/shard_map/pallas_call | solution.py:21
  47.9 2.2 %shard_map.83 = f32[16,8192]{1,0:T(8,128)} custom-call(s32[1,8192]{1,0:T(1,128)S(1)} %shard_map.73.refs_0_.comp_ref, bf16[16,256,256]{2,1,0:T(8,128)(2,1)S(1)} %copy-done.1, f32[512,256]{1,0:T(8,128)S(1)} %shard_map.82.start_ref, bf16[16,2048]{1,0:T(8,128)(2,1)S(1)} %get-tuple-element.46.refs_0_, bf16[16,2048]{1,0:T(8,128)(2,1)S(1)} %collective-permute-done.11.refs_1_), custom_call_target="tpu_custom_call" | custom-call | flops 2000000000 | bytes 1048576 | tf_op jit(solution)/shard_map/pallas_call | solution.py:21
  (20 shorter events, 0.3 us)
Async XLA Ops:
  0.0 4.7 %collective-permute-start = (bf16[16,8192]{1,0:T(8,128)(2,1)}, bf16[16,8192]{1,0:T(8,128)(2,1)S(1)}, u32[]{:S(2)}, u32[]{:S(2)}) collective-permute-start(bf16[16,8192]{1,0:T(8,128)(2,1)} %bitcast.10), channel_id=1, source_target_pairs={{0,1},{1,0},{2,3},{3,2},{4,5},{5,4},{6,7},{7,6},{8,9},{9,8},{10,11... | collective-permute-start | bytes 786440 | tf_op jit(solution)/shard_map/ppermute | solution.py:414
  1.0 3.7 %collective-permute-start.1 = (s32[12,16]{1,0:T(8,128)S(1)}, s32[12,16]{1,0:T(8,128)S(1)}, u32[]{:S(2)}, u32[]{:S(2)}) collective-permute-start(s32[12,16]{1,0:T(8,128)S(1)} %get-tuple-element.26.refs_0_), channel_id=1, source_target_pairs={{0,2},{2,0},{1,3},{3,1},{4,6},{6,4},{5,7},{7,5},{8,10},{10,8},{9,1... | collective-permute-start | bytes 2312 | tf_op jit(solution)/shard_map/ppermute | solution.py:414
  2.6 10.3 %collective-permute-start.2 = (bf16[2,64,512]{2,1,0:T(8,128)(2,1)S(1)}, bf16[2,64,512]{2,1,0:T(8,128)(2,1)S(1)}, u32[]{:S(2)}, u32[]{:S(2)}) collective-permute-start(bf16[2,64,512]{2,1,0:T(8,128)(2,1)S(1)} %get-tuple-element.29), channel_id=1, source_target_pairs={{0,4},{4,8},{8,12},{12,0},{1,5},{5,9},{9,13},{13,1},{2,6},{6,10},{... | collective-permute-start | bytes 393224 | tf_op jit(solution)/shard_map/ppermute | solution.py:454
  4.2 8.8 %copy-start = (bf16[16,512,64]{1,2,0:T(8,128)(2,1)S(1)}, bf16[16,512,64]{1,2,0:T(8,128)(2,1)}, u32[]{:S(2)}) copy-start(bf16[16,512,64]{1,2,0:T(8,128)(2,1)} %param.7) | copy-start | bytes 3145732
  4.2 8.8 %copy-start.2 = (s32[16,512]{1,0:T(8,128)S(1)}, s32[16,512]{1,0:T(8,128)}, u32[]{:S(2)}) copy-start(s32[16,512]{1,0:T(8,128)} %skel_ref.5) | copy-start | bytes 98308
  4.2 8.7 %collective-permute-start.3 = (bf16[2,64,512]{2,1,0:T(8,128)(2,1)S(1)}, bf16[2,64,512]{2,1,0:T(8,128)(2,1)S(1)}, u32[]{:S(2)}, u32[]{:S(2)}) collective-permute-start(bf16[2,64,512]{2,1,0:T(8,128)(2,1)S(1)} %get-tuple-element.30), channel_id=1, source_target_pairs={{0,12},{4,0},{8,4},{12,8},{1,13},{5,1},{9,5},{13,9},{2,14},{6,2},{... | collective-permute-start | bytes 393224 | tf_op jit(solution)/shard_map/ppermute | solution.py:455
  8.2 16.4 %collective-permute-start.4 = (bf16[400,256]{1,0:T(8,128)(2,1)S(1)}, bf16[400,256]{1,0:T(8,128)(2,1)S(1)}, u32[]{:S(2)}, u32[]{:S(2)}) collective-permute-start(bf16[400,256]{1,0:T(8,128)(2,1)S(1)} %get-tuple-element.34), channel_id=1, source_target_pairs={{0,4},{4,8},{8,12},{12,0},{1,5},{5,9},{9,13},{13,1},{2,6},{6,10},{... | collective-permute-start | bytes 614408 | tf_op jit(solution)/shard_map/ppermute | solution.py:484
  9.9 16.4 %collective-permute-start.5 = (bf16[400,256]{1,0:T(8,128)(2,1)S(1)}, bf16[400,256]{1,0:T(8,128)(2,1)S(1)}, u32[]{:S(2)}, u32[]{:S(2)}) collective-permute-start(bf16[400,256]{1,0:T(8,128)(2,1)S(1)} %get-tuple-element.35), channel_id=1, source_target_pairs={{0,12},{4,0},{8,4},{12,8},{1,13},{5,1},{9,5},{13,9},{2,14},{6,2},{... | collective-permute-start | bytes 614408 | tf_op jit(solution)/shard_map/ppermute | solution.py:484
  10.5 21.4 %collective-permute-start.8 = (bf16[384,256]{1,0:T(8,128)(2,1)S(1)}, bf16[384,256]{1,0:T(8,128)(2,1)S(1)}, u32[]{:S(2)}, u32[]{:S(2)}) collective-permute-start(bf16[384,256]{1,0:T(8,128)(2,1)S(1)} %get-tuple-element.39), channel_id=1, source_target_pairs={{0,8},{4,12},{8,0},{12,4},{1,9},{5,13},{9,1},{13,5},{2,10},{6,14},... | collective-permute-start | bytes 589832 | tf_op jit(solution)/shard_map/ppermute | solution.py:484
  31.8 1.6 %collective-permute-start.6 = (bf16[16,8192]{1,0:T(8,128)(2,1)S(1)}, bf16[16,8192]{1,0:T(8,128)(2,1)S(1)}, u32[]{:S(2)}, u32[]{:S(2)}) collective-permute-start(bf16[16,8192]{1,0:T(8,128)(2,1)S(1)} %get-tuple-element.37), channel_id=1, source_target_pairs={{0,1},{1,0},{2,3},{3,2},{4,5},{5,4},{6,7},{7,6},{8,9},{9,8},{10,11... | collective-permute-start | bytes 786440 | tf_op jit(solution)/shard_map/ppermute | solution.py:414
  33.5 8.4 %collective-permute-start.7 = (bf16[16,8192]{1,0:T(8,128)(2,1)S(1)}, bf16[16,8192]{1,0:T(8,128)(2,1)S(1)}, u32[]{:S(2)}, u32[]{:S(2)}) collective-permute-start(bf16[16,8192]{1,0:T(8,128)(2,1)S(1)} %add_convert_fusion.refs_0_.after_ref), channel_id=1, source_target_pairs={{0,2},{2,0},{1,3},{3,1},{4,6},{6,4},{5,7},{7,5},{8,10},{10,8},{9,1... | collective-permute-start | bytes 786440 | tf_op jit(solution)/shard_map/ppermute | solution.py:414
  33.6 4.1 %copy-start.3 = (s32[1,8192]{1,0:T(1,128)S(1)}, s32[1,8192]{1,0:T(1,128)}, u32[]{:S(2)}) copy-start(s32[1,8192]{1,0:T(1,128)} %order_ref.5) | copy-start | bytes 98308
  37.5 1.4 %collective-permute-start.9 = (bf16[16,4096]{1,0:T(8,128)(2,1)S(1)}, bf16[16,4096]{1,0:T(8,128)(2,1)S(1)}, u32[]{:S(2)}, u32[]{:S(2)}) collective-permute-start(bf16[16,4096]{1,0:T(8,128)(2,1)S(1)} %get-tuple-element.44), channel_id=1, source_target_pairs={{0,1},{1,0},{2,3},{3,2},{4,5},{5,4},{6,7},{7,6},{8,9},{9,8},{10,11... | collective-permute-start | bytes 393224 | tf_op jit(solution)/shard_map/ppermute | solution.py:414
  41.9 4.5 %collective-permute-start.10 = (bf16[16,2048]{1,0:T(8,128)(2,1)S(1)}, bf16[16,2048]{1,0:T(8,128)(2,1)S(1)}, u32[]{:S(2)}, u32[]{:S(2)}) collective-permute-start(bf16[16,2048]{1,0:T(8,128)(2,1)S(1)} %get-tuple-element.45.refs_0_), channel_id=1, source_target_pairs={{0,2},{2,0},{1,3},{3,1},{4,6},{6,4},{5,7},{7,5},{8,10},{10,8},{9,1... | collective-permute-start | bytes 196616 | tf_op jit(solution)/shard_map/ppermute | solution.py:414
  42.3 4.1 %copy-start.1 = (bf16[16,256,256]{2,1,0:T(8,128)(2,1)S(1)}, bf16[16,256,256]{2,1,0:T(8,128)(2,1)}, u32[]{:S(2)}) copy-start(bf16[16,256,256]{2,1,0:T(8,128)(2,1)} %interp_ref.5) | copy-start | bytes 6291460
  42.3 5.6 %collective-permute-start.11 = (bf16[16,2048]{1,0:T(8,128)(2,1)S(1)}, bf16[16,2048]{1,0:T(8,128)(2,1)S(1)}, u32[]{:S(2)}, u32[]{:S(2)}) collective-permute-start(bf16[16,2048]{1,0:T(8,128)(2,1)S(1)} %get-tuple-element.46.refs_0_), channel_id=1, source_target_pairs={{0,2},{2,0},{1,3},{3,1},{4,6},{6,4},{5,7},{7,5},{8,10},{10,8},{9,1... | collective-permute-start | bytes 196616 | tf_op jit(solution)/shard_map/ppermute | solution.py:414

commit v2 on v1

--- a/solution.py
+++ b/solution.py
@@ -191,18 +191,24 @@
     return found
 
 
-def named_sum(t, k, first, scale, cnt_ref, slots, at, tgt, src, weights, shift):
-    if k == 0:
-        return jnp.zeros((weights.shape[1], tgt.shape[2]), F32)
+def named_block(t, k, scale, slots, at, tgt, src, shift):
     names = [slots[at + j] for j in range(k)]
-    size = src.shape[1]
-    block = gauss(jnp.concatenate([src[s + shift] for s in names], axis=0), tgt[t], scale)
-    total = None
+    return names, gauss(jnp.concatenate([src[s + shift] for s in names], axis=0), tgt[t], scale) if k else None
+
+
+def named_product(t, first, cnt_ref, names, block, weights, shift, wide):
+    total = jnp.zeros((weights.shape[1], wide), F32) if not names else None
     for j, s in enumerate(names):
+        size = weights.shape[2]
         times = cnt_ref[first + s, t].astype(F32)
         part = dot(weights[s + shift], block[j * size : (j + 1) * size]) * times
         total = part if total is None else total + part
     return total
+
+
+def named_sum(t, k, first, scale, cnt_ref, slots, at, tgt, src, weights, shift):
+    names, block = named_block(t, k, scale, slots, at, tgt, src, shift)
+    return named_product(t, first, cnt_ref, names, block, weights, shift, tgt.shape[2])
 
 
 def near_body(
@@ -267,9 +273,13 @@
 
             @pl.when((founds[0] == counts[0]) & (founds[1] == counts[1]))
             def _():
+                blocks = [
+                    named_block(t, c, scale, slots, n * (halo + 1), tgt_ref, src, right * halo)
+                    for n, (t, c) in enumerate(zip(pair, counts))
+                ]
                 sums = [
-                    named_sum(t, c, first, scale, cnt_ref, slots, n * (halo + 1), tgt_ref, src, wts, right * halo)
-                    for n, (t, c) in enumerate(zip(pair, counts))
+                    named_product(t, first, cnt_ref, names, block, wts, right * halo, size)
+                    for t, (names, block) in zip(pair, blocks)
                 ]
                 totals = [near_ref[t] + part for t, part in zip(pair, sums)]
                 for t, total in zip(pair, totals):

time: 50.3 us -> 49.9 us (level)
  transfers between devices with their start and end apart: 12 -> 12, of which waited for: 5 -> 4; matrix products, arithmetic and copies ran while one was open for 0% -> 0% of each run, Pallas kernels for 62% -> 62%
where the time goes in v2:
time: 49.9 us; the launch traced here: 49.8 us
  Pallas kernels  33.3 us (67%)
  starting transfers between devices  10.7 us (21%)
  waiting for transfers between devices  5.53 us (11%)
    pallas_call x11, Pallas kernels, call(): pl.pallas_call(body, out_shape=outs, in_specs=specs, out_specs=out_specs...  33.3 us
    ppermute x3, starting transfers between devices, on_device(): lax.ppermute(outgoing[by], 'leaf', ring(blocks, by))  4.67 us
    ppermute x7, starting transfers between devices, from_others(): lax.ppermute(value, axis, ring(count, by))  4.01 us
    ppermute x7, waiting for transfers between devices, from_others(): lax.ppermute(value, axis, ring(count, by))  3.98 us
    ppermute x1, starting transfers between devices, on_device(): left_p = lax.ppermute(up_p, 'leaf', ring(blocks, 1))  1.58 us
    ppermute x3, waiting for transfers between devices, on_device(): lax.ppermute(outgoing[by], 'leaf', ring(blocks, by))  1.55 us
  transfers between devices with their start and end apart: 12, of which 4 were waited for; matrix products, arithmetic and copies ran while one was open for 0% of the time, Pallas kernels for 62%

profile of v2, /device:TPU:8, one launch (start us, length us, event | category | flops | bytes accessed | tf_op | source)
XLA Modules:
  0.0 49.8 jit_solution(409931423268485474)
XLA Ops:
  0.0 1.0 %shard_map.74 = (bf16[2,64,512]{2,1,0:T(8,128)(2,1)S(1)}, bf16[2,64,512]{2,1,0:T(8,128)(2,1)S(1)}, s32[12,16]{1,0:T(8,128)S(1)}) custom-call(bf16[16,64,512]{2,1,0:T(8,128)(2,1)} %bitcast.5, s32[8,16]{1,0:T(8,128)} %bitcast.8, s32[4,16]{1,0:T(4,128)} %bitcast.9), custom_call_target="tpu_custom_call" | custom-call | bytes 1048576 | tf_op jit(solution)/shard_map/pallas_call | solution.py:21
  1.0 1.6 %collective-permute-start.1 = (s32[12,16]{1,0:T(8,128)S(1)}, s32[12,16]{1,0:T(8,128)S(1)}, u32[]{:S(2)}, u32[]{:S(2)}) collective-permute-start(s32[12,16]{1,0:T(8,128)S(1)} %get-tuple-element.26.refs_0_), channel_id=1, source_target_pairs={{0,2},{2,0},{1,3},{3,1},{4,6},{6,4},{5,7},{7,5},{8,10},{10,8},{9,1... | collective-permute-start | bytes 2312 | tf_op jit(solution)/shard_map/ppermute | solution.py:424
  2.6 1.6 %collective-permute-start.2 = (bf16[2,64,512]{2,1,0:T(8,128)(2,1)S(1)}, bf16[2,64,512]{2,1,0:T(8,128)(2,1)S(1)}, u32[]{:S(2)}, u32[]{:S(2)}) collective-permute-start(bf16[2,64,512]{2,1,0:T(8,128)(2,1)S(1)} %get-tuple-element.29), channel_id=1, source_target_pairs={{0,4},{4,8},{8,12},{12,0},{1,5},{5,9},{9,13},{13,1},{2,6},{6,10},{... | collective-permute-start | bytes 393224 | tf_op jit(solution)/shard_map/ppermute | solution.py:464
  4.2 0.4 collective-permute-start.3
  4.6 0.1 collective-permute-done.1.refs_1_
  4.7 3.5 %shard_map.75 = (bf16[4,32,512]{2,1,0:T(8,128)(2,1)S(1)}, bf16[400,256]{1,0:T(8,128)(2,1)S(1)}, bf16[384,256]{1,0:T(8,128)(2,1)S(1)}, bf16[400,256]{1,0:T(8,128)...) custom-call(bf16[16,8192]{1,0:T(8,128)(2,1)} %bitcast.11, bf16[16,8192]{1,0:T(8,128)(2,1)S(1)} %collective-permute-done.other_ref, ...), custom_call_target="tpu_custom_call" | custom-call | flops 3000000000 | bytes 1048576 | tf_op jit(solution)/shard_map/pallas_call | solution.py:21
  8.2 1.6 %collective-permute-start.4 = (bf16[400,256]{1,0:T(8,128)(2,1)S(1)}, bf16[400,256]{1,0:T(8,128)(2,1)S(1)}, u32[]{:S(2)}, u32[]{:S(2)}) collective-permute-start(bf16[400,256]{1,0:T(8,128)(2,1)S(1)} %get-tuple-element.34), channel_id=1, source_target_pairs={{0,4},{4,8},{8,12},{12,0},{1,5},{5,9},{9,13},{13,1},{2,6},{6,10},{... | collective-permute-start | bytes 614408 | tf_op jit(solution)/shard_map/ppermute | solution.py:494
  9.9 0.6 %collective-permute-start.5 = (bf16[400,256]{1,0:T(8,128)(2,1)S(1)}, bf16[400,256]{1,0:T(8,128)(2,1)S(1)}, u32[]{:S(2)}, u32[]{:S(2)}) collective-permute-start(bf16[400,256]{1,0:T(8,128)(2,1)S(1)} %get-tuple-element.35), channel_id=1, source_target_pairs={{0,12},{4,0},{8,4},{12,8},{1,13},{5,1},{9,5},{13,9},{2,14},{6,2},{... | collective-permute-start | bytes 614408 | tf_op jit(solution)/shard_map/ppermute | solution.py:494
  10.5 2.4 %collective-permute-start.8 = (bf16[384,256]{1,0:T(8,128)(2,1)S(1)}, bf16[384,256]{1,0:T(8,128)(2,1)S(1)}, u32[]{:S(2)}, u32[]{:S(2)}) collective-permute-start(bf16[384,256]{1,0:T(8,128)(2,1)S(1)} %get-tuple-element.39), channel_id=1, source_target_pairs={{0,8},{4,12},{8,0},{12,4},{1,9},{5,13},{9,1},{13,5},{2,10},{6,14},... | collective-permute-start | bytes 589832 | tf_op jit(solution)/shard_map/ppermute | solution.py:494
  12.9 11.7 %shard_map.76 = (f32[16,32,512]{2,1,0:T(8,128)S(1)}, bf16[16,80,512]{2,1,0:T(8,128)(2,1)S(1)}, bf16[4,512,80]{2,1,0:T(8,128)(2,1)S(1)}, bf16[16,80,256]{2,1,0:T(8,128)(2,1)S(1)}) custom-call(s32[8,16]{1,0:T(8,128)S(1)} %get-tuple-element.27.cnt_ref, bf16[16,64,512]{2,1,0:T(8,128)(2,1)S(1)} %bitcast.7, bf16[4,32,512]{2,1,0:T(8,128)(2,1)S(1)} %get-tuple-element.28.tw_ref, ...), custom_call_target="tpu_custom_call" | custom-call | flops 14000000000 | bytes 1048576 | tf_op jit(solution)/shard_map/pallas_call | solution.py:21
  24.7 1.5 %collective-permute-done.5.right_m.refs_2_ = bf16[400,256]{1,0:T(8,128)(2,1)S(1)} collective-permute-done((bf16[400,256]{1,0:T(8,128)(2,1)S(1)}, bf16[400,256]{1,0:T(8,128)(2,1)S(1)}, u32[]{:S(2)}, u32[]{:S(2)}) %collective-permute-start.5) | collective-permute-done | bytes 204832 | tf_op jit(solution)/shard_map/ppermute | solution.py:494
  26.2 5.2 %shard_map.77 = (f32[16,8192]{1,0:T(8,128)S(1)}, bf16[16,8192]{1,0:T(8,128)(2,1)S(1)}) custom-call(s32[8,16]{1,0:T(8,128)S(1)} %get-tuple-element.27.cnt_ref, f32[16,32,512]{2,1,0:T(8,128)S(1)} %get-tuple-element.31.near_ref, bf16[16,80,512]{2,1,0:T(8,128)(2,1)S(1)} %get-tuple-element.32.tgt_ref, bf16[4,512,80]{2,1,0:T(8,128)(2,1)S(1)} %get-tuple-element.33.src, ...), custom_call_target="tpu_custom_call" | custom-call | flops 6000000000 | bytes 1048576 | tf_op jit(solution)/shard_map/pallas_call | solution.py:21
  31.5 0.5 %shard_map.79 = (bf16[12,256,80]{2,1,0:T(8,128)(2,1)S(1)}, bf16[12,32,256]{2,1,0:T(8,128)(2,1)S(1)}) custom-call(bf16[2,64,512]{2,1,0:T(8,128)(2,1)S(1)} %collective-permute-done.2.left_p, bf16[2,64,512]{2,1,0:T(8,128)(2,1)S(1)} %collective-permute-done.3.right_p, bf16[400,256]{1,0:T(8,128)(2,1)S(1)} %collective-permute-done.4.left_m.refs_0_, ...), custom_call_target="tpu_custom_call" | custom-call | flops 2000000000 | bytes 1048576 | tf_op jit(solution)/shard_map/pallas_call | solution.py:21
  32.1 1.0 %collective-permute-done.6 = bf16[16,8192]{1,0:T(8,128)(2,1)S(1)} collective-permute-done((bf16[16,8192]{1,0:T(8,128)(2,1)S(1)}, bf16[16,8192]{1,0:T(8,128)(2,1)S(1)}, u32[]{:S(2)}, u32[]{:S(2)}) %collective-permute-start.6) | collective-permute-done | bytes 262176 | tf_op jit(solution)/shard_map/ppermute | solution.py:424
  33.1 0.1 collective-permute-start.7
  33.2 4.0 %shard_map.80 = (f32[16,4096]{1,0:T(8,128)S(1)}, bf16[16,4096]{1,0:T(8,128)(2,1)S(1)}) custom-call(s32[8,16]{1,0:T(8,128)S(1)} %get-tuple-element.38.far_ref, bf16[12,256,80]{2,1,0:T(8,128)(2,1)S(1)} %get-tuple-element.40.far_src, bf16[12,32,256]{2,1,0:T(8,128)(2,1)S(1)} %get-tuple-element.41.far_w, bf16[16,80,256]{2,1,0:T(8,128)(2,1)S(1)} %get-tuple-element.42.far_tgt, ...), custom_call_target="tpu_custom_call" | custom-call | flops 4000000000 | bytes 1048576 | tf_op jit(solution)/shard_map/pallas_call | solution.py:21
  37.2 0.2 collective-permute-start.9
  37.4 1.2 %shard_map.73.refs_0_.comp_ref = s32[1,8192]{1,0:T(1,128)S(1)} custom-call(s32[1,8192]{1,0:T(1,128)S(1)} %copy-done.3, s32[16,512]{1,0:T(8,128)S(1)} %copy-done.2), custom_call_target="tpu_custom_call" | custom-call | flops 1000000000 | bytes 1048576 | tf_op jit(solution)/shard_map/pallas_call | solution.py:21
  38.6 2.9 %collective-permute-done.7.refs_1_ = bf16[16,8192]{1,0:T(8,128)(2,1)S(1)} collective-permute-done((bf16[16,8192]{1,0:T(8,128)(2,1)S(1)}, bf16[16,8192]{1,0:T(8,128)(2,1)S(1)}, u32[]{:S(2)}, u32[]{:S(2)}) %collective-permute-start.7) | collective-permute-done | bytes 262176 | tf_op jit(solution)/shard_map/ppermute | solution.py:424
  41.6 0.4 collective-permute-start.10
  41.9 1.7 %collective-permute-start.11 = (bf16[16,2048]{1,0:T(8,128)(2,1)S(1)}, bf16[16,2048]{1,0:T(8,128)(2,1)S(1)}, u32[]{:S(2)}, u32[]{:S(2)}) collective-permute-start(bf16[16,2048]{1,0:T(8,128)(2,1)S(1)} %get-tuple-element.46.refs_0_), channel_id=1, source_target_pairs={{0,2},{2,0},{1,3},{3,1},{4,6},{6,4},{5,7},{7,5},{8,10},{10,8},{9,1... | collective-permute-start | bytes 196616 | tf_op jit(solution)/shard_map/ppermute | solution.py:424
  43.7 2.4 %shard_map.78.start_ref = f32[512,256]{1,0:T(8,128)S(1)} custom-call(s32[1,8192]{1,0:T(1,128)S(1)} %copy-done.3, bf16[16,8192]{1,0:T(8,128)(2,1)S(1)} %add_convert_fusion.refs_0_.after_ref, bf16[16,8192]{1,0:T(8,128)(2,1)S(1)} %collective-permute-done.7.refs_1_), custom_call_target="tpu_custom_call" | custom-call | flops 3000000000 | bytes 1048576 | tf_op jit(solution)/shard_map/pallas_call | solution.py:21
  46.0 1.4 %shard_map.82.start_ref = f32[512,256]{1,0:T(8,128)S(1)} custom-call(s32[1,8192]{1,0:T(1,128)S(1)} %shard_map.73.refs_0_.comp_ref, bf16[16,256,256]{2,1,0:T(8,128)(2,1)S(1)} %copy-done.1, f32[512,256]{1,0:T(8,128)S(1)} %shard_map.78.start_ref, bf16[16,2048]{1,0:T(8,128)(2,1)S(1)} %get-tuple-element.45.refs_0_, ...), custom_call_target="tpu_custom_call" | custom-call | flops 2000000000 | bytes 1048576 | tf_op jit(solution)/shard_map/pallas_call | solution.py:21
  47.5 2.2 %shard_map.83 = f32[16,8192]{1,0:T(8,128)} custom-call(s32[1,8192]{1,0:T(1,128)S(1)} %shard_map.73.refs_0_.comp_ref, bf16[16,256,256]{2,1,0:T(8,128)(2,1)S(1)} %copy-done.1, f32[512,256]{1,0:T(8,128)S(1)} %shard_map.82.start_ref, bf16[16,2048]{1,0:T(8,128)(2,1)S(1)} %get-tuple-element.46.refs_0_, bf16[16,2048]{1,0:T(8,128)(2,1)S(1)} %collective-permute-done.11.refs_1_), custom_call_target="tpu_custom_call" | custom-call | flops 2000000000 | bytes 1048576 | tf_op jit(solution)/shard_map/pallas_call | solution.py:21
  (20 shorter events, 0.2 us)
Async XLA Ops:
  0.0 4.7 %collective-permute-start = (bf16[16,8192]{1,0:T(8,128)(2,1)}, bf16[16,8192]{1,0:T(8,128)(2,1)S(1)}, u32[]{:S(2)}, u32[]{:S(2)}) collective-permute-start(bf16[16,8192]{1,0:T(8,128)(2,1)} %bitcast.10), channel_id=1, source_target_pairs={{0,1},{1,0},{2,3},{3,2},{4,5},{5,4},{6,7},{7,6},{8,9},{9,8},{10,11... | collective-permute-start | bytes 786440 | tf_op jit(solution)/shard_map/ppermute | solution.py:424
  1.0 3.7 %collective-permute-start.1 = (s32[12,16]{1,0:T(8,128)S(1)}, s32[12,16]{1,0:T(8,128)S(1)}, u32[]{:S(2)}, u32[]{:S(2)}) collective-permute-start(s32[12,16]{1,0:T(8,128)S(1)} %get-tuple-element.26.refs_0_), channel_id=1, source_target_pairs={{0,2},{2,0},{1,3},{3,1},{4,6},{6,4},{5,7},{7,5},{8,10},{10,8},{9,1... | collective-permute-start | bytes 2312 | tf_op jit(solution)/shard_map/ppermute | solution.py:424
  2.6 10.3 %collective-permute-start.2 = (bf16[2,64,512]{2,1,0:T(8,128)(2,1)S(1)}, bf16[2,64,512]{2,1,0:T(8,128)(2,1)S(1)}, u32[]{:S(2)}, u32[]{:S(2)}) collective-permute-start(bf16[2,64,512]{2,1,0:T(8,128)(2,1)S(1)} %get-tuple-element.29), channel_id=1, source_target_pairs={{0,4},{4,8},{8,12},{12,0},{1,5},{5,9},{9,13},{13,1},{2,6},{6,10},{... | collective-permute-start | bytes 393224 | tf_op jit(solution)/shard_map/ppermute | solution.py:464
  4.2 8.8 %copy-start = (bf16[16,512,64]{1,2,0:T(8,128)(2,1)S(1)}, bf16[16,512,64]{1,2,0:T(8,128)(2,1)}, u32[]{:S(2)}) copy-start(bf16[16,512,64]{1,2,0:T(8,128)(2,1)} %param.7) | copy-start | bytes 3145732
  4.2 8.8 %copy-start.2 = (s32[16,512]{1,0:T(8,128)S(1)}, s32[16,512]{1,0:T(8,128)}, u32[]{:S(2)}) copy-start(s32[16,512]{1,0:T(8,128)} %skel_ref.5) | copy-start | bytes 98308
  4.2 8.7 %collective-permute-start.3 = (bf16[2,64,512]{2,1,0:T(8,128)(2,1)S(1)}, bf16[2,64,512]{2,1,0:T(8,128)(2,1)S(1)}, u32[]{:S(2)}, u32[]{:S(2)}) collective-permute-start(bf16[2,64,512]{2,1,0:T(8,128)(2,1)S(1)} %get-tuple-element.30), channel_id=1, source_target_pairs={{0,12},{4,0},{8,4},{12,8},{1,13},{5,1},{9,5},{13,9},{2,14},{6,2},{... | collective-permute-start | bytes 393224 | tf_op jit(solution)/shard_map/ppermute | solution.py:465
  8.2 16.4 %collective-permute-start.4 = (bf16[400,256]{1,0:T(8,128)(2,1)S(1)}, bf16[400,256]{1,0:T(8,128)(2,1)S(1)}, u32[]{:S(2)}, u32[]{:S(2)}) collective-permute-start(bf16[400,256]{1,0:T(8,128)(2,1)S(1)} %get-tuple-element.34), channel_id=1, source_target_pairs={{0,4},{4,8},{8,12},{12,0},{1,5},{5,9},{9,13},{13,1},{2,6},{6,10},{... | collective-permute-start | bytes 614408 | tf_op jit(solution)/shard_map/ppermute | solution.py:494
  9.9 16.4 %collective-permute-start.5 = (bf16[400,256]{1,0:T(8,128)(2,1)S(1)}, bf16[400,256]{1,0:T(8,128)(2,1)S(1)}, u32[]{:S(2)}, u32[]{:S(2)}) collective-permute-start(bf16[400,256]{1,0:T(8,128)(2,1)S(1)} %get-tuple-element.35), channel_id=1, source_target_pairs={{0,12},{4,0},{8,4},{12,8},{1,13},{5,1},{9,5},{13,9},{2,14},{6,2},{... | collective-permute-start | bytes 614408 | tf_op jit(solution)/shard_map/ppermute | solution.py:494
  10.5 21.0 %collective-permute-start.8 = (bf16[384,256]{1,0:T(8,128)(2,1)S(1)}, bf16[384,256]{1,0:T(8,128)(2,1)S(1)}, u32[]{:S(2)}, u32[]{:S(2)}) collective-permute-start(bf16[384,256]{1,0:T(8,128)(2,1)S(1)} %get-tuple-element.39), channel_id=1, source_target_pairs={{0,8},{4,12},{8,0},{12,4},{1,9},{5,13},{9,1},{13,5},{2,10},{6,14},... | collective-permute-start | bytes 589832 | tf_op jit(solution)/shard_map/ppermute | solution.py:494
  31.4 1.6 %collective-permute-start.6 = (bf16[16,8192]{1,0:T(8,128)(2,1)S(1)}, bf16[16,8192]{1,0:T(8,128)(2,1)S(1)}, u32[]{:S(2)}, u32[]{:S(2)}) collective-permute-start(bf16[16,8192]{1,0:T(8,128)(2,1)S(1)} %get-tuple-element.37), channel_id=1, source_target_pairs={{0,1},{1,0},{2,3},{3,2},{4,5},{5,4},{6,7},{7,6},{8,9},{9,8},{10,11... | collective-permute-start | bytes 786440 | tf_op jit(solution)/shard_map/ppermute | solution.py:424
  33.1 8.4 %collective-permute-start.7 = (bf16[16,8192]{1,0:T(8,128)(2,1)S(1)}, bf16[16,8192]{1,0:T(8,128)(2,1)S(1)}, u32[]{:S(2)}, u32[]{:S(2)}) collective-permute-start(bf16[16,8192]{1,0:T(8,128)(2,1)S(1)} %add_convert_fusion.refs_0_.after_ref), channel_id=1, source_target_pairs={{0,2},{2,0},{1,3},{3,1},{4,6},{6,4},{5,7},{7,5},{8,10},{10,8},{9,1... | collective-permute-start | bytes 786440 | tf_op jit(solution)/shard_map/ppermute | solution.py:424
  33.2 4.2 %copy-start.3 = (s32[1,8192]{1,0:T(1,128)S(1)}, s32[1,8192]{1,0:T(1,128)}, u32[]{:S(2)}) copy-start(s32[1,8192]{1,0:T(1,128)} %order_ref.5) | copy-start | bytes 98308
  37.2 1.4 %collective-permute-start.9 = (bf16[16,4096]{1,0:T(8,128)(2,1)S(1)}, bf16[16,4096]{1,0:T(8,128)(2,1)S(1)}, u32[]{:S(2)}, u32[]{:S(2)}) collective-permute-start(bf16[16,4096]{1,0:T(8,128)(2,1)S(1)} %get-tuple-element.44), channel_id=1, source_target_pairs={{0,1},{1,0},{2,3},{3,2},{4,5},{5,4},{6,7},{7,6},{8,9},{9,8},{10,11... | collective-permute-start | bytes 393224 | tf_op jit(solution)/shard_map/ppermute | solution.py:424
  41.6 4.5 %collective-permute-start.10 = (bf16[16,2048]{1,0:T(8,128)(2,1)S(1)}, bf16[16,2048]{1,0:T(8,128)(2,1)S(1)}, u32[]{:S(2)}, u32[]{:S(2)}) collective-permute-start(bf16[16,2048]{1,0:T(8,128)(2,1)S(1)} %get-tuple-element.45.refs_0_), channel_id=1, source_target_pairs={{0,2},{2,0},{1,3},{3,1},{4,6},{6,4},{5,7},{7,5},{8,10},{10,8},{9,1... | collective-permute-start | bytes 196616 | tf_op jit(solution)/shard_map/ppermute | solution.py:424
  41.9 4.1 %copy-start.1 = (bf16[16,256,256]{2,1,0:T(8,128)(2,1)S(1)}, bf16[16,256,256]{2,1,0:T(8,128)(2,1)}, u32[]{:S(2)}) copy-start(bf16[16,256,256]{2,1,0:T(8,128)(2,1)} %interp_ref.5) | copy-start | bytes 6291460
  41.9 5.6 %collective-permute-start.11 = (bf16[16,2048]{1,0:T(8,128)(2,1)S(1)}, bf16[16,2048]{1,0:T(8,128)(2,1)S(1)}, u32[]{:S(2)}, u32[]{:S(2)}) collective-permute-start(bf16[16,2048]{1,0:T(8,128)(2,1)S(1)} %get-tuple-element.46.refs_0_), channel_id=1, source_target_pairs={{0,2},{2,0},{1,3},{3,1},{4,6},{6,4},{5,7},{7,5},{8,10},{10,8},{9,1... | collective-permute-start | bytes 196616 | tf_op jit(solution)/shard_map/ppermute | solution.py:424

commit v3 on v2

--- a/solution.py
+++ b/solution.py
@@ -206,11 +206,6 @@
     return total
 
 
-def named_sum(t, k, first, scale, cnt_ref, slots, at, tgt, src, weights, shift):
-    names, block = named_block(t, k, scale, slots, at, tgt, src, shift)
-    return named_product(t, first, cnt_ref, names, block, weights, shift, tgt.shape[2])
-
-
 def near_body(
     halo, scale, cnt_ref, pts_ref, tw_ref, left_p, right_p, skel_ref,
     near_ref, tgt_ref, edge_src, far_tgt_ref, src, slots,
@@ -233,12 +228,12 @@
 
             @pl.when(found == k)
             def _():
-                total = named_sum(t, k, halo, scale, cnt_ref, slots, 0, tgt_ref, src, tw_ref, 0)
+                names, block = named_block(t, k, scale, slots, 0, tgt_ref, src, 0)
                 hot = one_hot(skel_ref[pl.ds(t, 1), :rank], size)
                 far_tgt = as_targets(dot(pts_ref[t], hot).astype(BF))
                 later = jnp.minimum(t + 1, leaves - 1)
                 following = as_targets(pts_ref[later])
-                near_ref[t] = total
+                near_ref[t] = named_product(t, halo, cnt_ref, names, block, tw_ref, 0, size)
                 far_tgt_ref[t] = far_tgt
                 tgt_ref[later] = following
 

time: 49.9 us -> 49.4 us (0.990); the launches traced: 49.8 us -> 48.7 us
  waiting for transfers between devices: 5.53 us -> 4.1 us
  starting transfers between devices: 10.7 us -> 11.5 us
    ppermute x3, waiting for transfers between devices: 1.55 us -> 0.39 us  [on_device(): lax.ppermute(outgoing[by], 'leaf', ring(blocks, by))]
    ppermute x7, starting transfers between devices: 4.01 us -> 4.85 us  [from_others(): lax.ppermute(value, axis, ring(count, by))]
  transfers between devices with their start and end apart: 12 -> 12, of which waited for: 4 -> 4; matrix products, arithmetic and copies ran while one was open for 0% -> 0% of each run, Pallas kernels for 62% -> 63%
where the time goes in v3:
time: 49.4 us; the launch traced here: 48.7 us
  Pallas kernels  32.9 us (67%)
  starting transfers between devices  11.5 us (23%)
  waiting for transfers between devices  4.1 us (8%)
    pallas_call x11, Pallas kernels, call(): pl.pallas_call(body, out_shape=outs, in_specs=specs, out_specs=out_specs...  32.9 us
    ppermute x7, starting transfers between devices, from_others(): lax.ppermute(value, axis, ring(count, by))  4.85 us
    ppermute x3, starting transfers between devices, on_device(): lax.ppermute(outgoing[by], 'leaf', ring(blocks, by))  4.67 us
    ppermute x7, waiting for transfers between devices, from_others(): lax.ppermute(value, axis, ring(count, by))  3.71 us
    ppermute x1, starting transfers between devices, on_device(): left_p = lax.ppermute(up_p, 'leaf', ring(blocks, 1))  1.58 us
  transfers between devices with their start and end apart: 12, of which 4 were waited for; matrix products, arithmetic and copies ran while one was open for 0% of the time, Pallas kernels for 63%

profile of v3, /device:TPU:8, one launch (start us, length us, event | category | flops | bytes accessed | tf_op | source)
XLA Modules:
  0.0 48.7 jit_solution(10413895665878264797)
XLA Ops:
  0.0 1.0 %shard_map.74 = (bf16[2,64,512]{2,1,0:T(8,128)(2,1)S(1)}, bf16[2,64,512]{2,1,0:T(8,128)(2,1)S(1)}, s32[12,16]{1,0:T(8,128)S(1)}) custom-call(bf16[16,64,512]{2,1,0:T(8,128)(2,1)} %bitcast.5, s32[8,16]{1,0:T(8,128)} %bitcast.8, s32[4,16]{1,0:T(4,128)} %bitcast.9), custom_call_target="tpu_custom_call" | custom-call | bytes 1048576 | tf_op jit(solution)/shard_map/pallas_call | solution.py:21
  1.0 1.6 %collective-permute-start.1 = (s32[12,16]{1,0:T(8,128)S(1)}, s32[12,16]{1,0:T(8,128)S(1)}, u32[]{:S(2)}, u32[]{:S(2)}) collective-permute-start(s32[12,16]{1,0:T(8,128)S(1)} %get-tuple-element.26.refs_0_), channel_id=1, source_target_pairs={{0,2},{2,0},{1,3},{3,1},{4,6},{6,4},{5,7},{7,5},{8,10},{10,8},{9,1... | collective-permute-start | bytes 2312 | tf_op jit(solution)/shard_map/ppermute | solution.py:419
  2.6 1.6 %collective-permute-start.2 = (bf16[2,64,512]{2,1,0:T(8,128)(2,1)S(1)}, bf16[2,64,512]{2,1,0:T(8,128)(2,1)S(1)}, u32[]{:S(2)}, u32[]{:S(2)}) collective-permute-start(bf16[2,64,512]{2,1,0:T(8,128)(2,1)S(1)} %get-tuple-element.29), channel_id=1, source_target_pairs={{0,4},{4,8},{8,12},{12,0},{1,5},{5,9},{9,13},{13,1},{2,6},{6,10},{... | collective-permute-start | bytes 393224 | tf_op jit(solution)/shard_map/ppermute | solution.py:459
  4.2 0.4 collective-permute-start.3
  4.6 0.1 collective-permute-done.1.refs_1_
  4.7 3.5 %shard_map.75 = (bf16[4,32,512]{2,1,0:T(8,128)(2,1)S(1)}, bf16[400,256]{1,0:T(8,128)(2,1)S(1)}, bf16[384,256]{1,0:T(8,128)(2,1)S(1)}, bf16[400,256]{1,0:T(8,128)...) custom-call(bf16[16,8192]{1,0:T(8,128)(2,1)} %bitcast.11, bf16[16,8192]{1,0:T(8,128)(2,1)S(1)} %collective-permute-done.other_ref, ...), custom_call_target="tpu_custom_call" | custom-call | flops 3000000000 | bytes 1048576 | tf_op jit(solution)/shard_map/pallas_call | solution.py:21
  8.2 1.6 %collective-permute-start.4 = (bf16[400,256]{1,0:T(8,128)(2,1)S(1)}, bf16[400,256]{1,0:T(8,128)(2,1)S(1)}, u32[]{:S(2)}, u32[]{:S(2)}) collective-permute-start(bf16[400,256]{1,0:T(8,128)(2,1)S(1)} %get-tuple-element.34), channel_id=1, source_target_pairs={{0,4},{4,8},{8,12},{12,0},{1,5},{5,9},{9,13},{13,1},{2,6},{6,10},{... | collective-permute-start | bytes 614408 | tf_op jit(solution)/shard_map/ppermute | solution.py:489
  9.9 0.6 %collective-permute-start.5 = (bf16[400,256]{1,0:T(8,128)(2,1)S(1)}, bf16[400,256]{1,0:T(8,128)(2,1)S(1)}, u32[]{:S(2)}, u32[]{:S(2)}) collective-permute-start(bf16[400,256]{1,0:T(8,128)(2,1)S(1)} %get-tuple-element.35), channel_id=1, source_target_pairs={{0,12},{4,0},{8,4},{12,8},{1,13},{5,1},{9,5},{13,9},{2,14},{6,2},{... | collective-permute-start | bytes 614408 | tf_op jit(solution)/shard_map/ppermute | solution.py:489
  10.5 2.4 %collective-permute-start.8 = (bf16[384,256]{1,0:T(8,128)(2,1)S(1)}, bf16[384,256]{1,0:T(8,128)(2,1)S(1)}, u32[]{:S(2)}, u32[]{:S(2)}) collective-permute-start(bf16[384,256]{1,0:T(8,128)(2,1)S(1)} %get-tuple-element.39), channel_id=1, source_target_pairs={{0,8},{4,12},{8,0},{12,4},{1,9},{5,13},{9,1},{13,5},{2,10},{6,14},... | collective-permute-start | bytes 589832 | tf_op jit(solution)/shard_map/ppermute | solution.py:489
  12.9 12.9 %shard_map.76 = (f32[16,32,512]{2,1,0:T(8,128)S(1)}, bf16[16,80,512]{2,1,0:T(8,128)(2,1)S(1)}, bf16[4,512,80]{2,1,0:T(8,128)(2,1)S(1)}, bf16[16,80,256]{2,1,0:T(8,128)(2,1)S(1)}) custom-call(s32[8,16]{1,0:T(8,128)S(1)} %get-tuple-element.27.cnt_ref, bf16[16,64,512]{2,1,0:T(8,128)(2,1)S(1)} %bitcast.7, bf16[4,32,512]{2,1,0:T(8,128)(2,1)S(1)} %get-tuple-element.28.tw_ref, ...), custom_call_target="tpu_custom_call" | custom-call | flops 14000000000 | bytes 1048576 | tf_op jit(solution)/shard_map/pallas_call | solution.py:21
  25.8 0.4 collective-permute-done.5.right_m.refs_2_
  26.2 4.2 %shard_map.77 = (f32[16,8192]{1,0:T(8,128)S(1)}, bf16[16,8192]{1,0:T(8,128)(2,1)S(1)}) custom-call(s32[8,16]{1,0:T(8,128)S(1)} %get-tuple-element.27.cnt_ref, f32[16,32,512]{2,1,0:T(8,128)S(1)} %get-tuple-element.31.near_ref, bf16[16,80,512]{2,1,0:T(8,128)(2,1)S(1)} %get-tuple-element.32.tgt_ref, bf16[4,512,80]{2,1,0:T(8,128)(2,1)S(1)} %get-tuple-element.33.src, ...), custom_call_target="tpu_custom_call" | custom-call | flops 6000000000 | bytes 1048576 | tf_op jit(solution)/shard_map/pallas_call | solution.py:21
  30.5 0.5 %shard_map.79 = (bf16[12,256,80]{2,1,0:T(8,128)(2,1)S(1)}, bf16[12,32,256]{2,1,0:T(8,128)(2,1)S(1)}) custom-call(bf16[2,64,512]{2,1,0:T(8,128)(2,1)S(1)} %collective-permute-done.2.left_p, bf16[2,64,512]{2,1,0:T(8,128)(2,1)S(1)} %collective-permute-done.3.right_p, bf16[400,256]{1,0:T(8,128)(2,1)S(1)} %collective-permute-done.4.left_m.refs_0_, ...), custom_call_target="tpu_custom_call" | custom-call | flops 2000000000 | bytes 1048576 | tf_op jit(solution)/shard_map/pallas_call | solution.py:21
  31.1 1.0 %collective-permute-done.6 = bf16[16,8192]{1,0:T(8,128)(2,1)S(1)} collective-permute-done((bf16[16,8192]{1,0:T(8,128)(2,1)S(1)}, bf16[16,8192]{1,0:T(8,128)(2,1)S(1)}, u32[]{:S(2)}, u32[]{:S(2)}) %collective-permute-start.6) | collective-permute-done | bytes 262176 | tf_op jit(solution)/shard_map/ppermute | solution.py:419
  32.1 0.6 %collective-permute-start.7 = (bf16[16,8192]{1,0:T(8,128)(2,1)S(1)}, bf16[16,8192]{1,0:T(8,128)(2,1)S(1)}, u32[]{:S(2)}, u32[]{:S(2)}) collective-permute-start(bf16[16,8192]{1,0:T(8,128)(2,1)S(1)} %add_convert_fusion.refs_0_.after_ref), channel_id=1, source_target_pairs={{0,2},{2,0},{1,3},{3,1},{4,6},{6,4},{5,7},{7,5},{8,10},{10,8},{9,1... | collective-permute-start | bytes 786440 | tf_op jit(solution)/shard_map/ppermute | solution.py:419
  32.8 3.4 %shard_map.80 = (f32[16,4096]{1,0:T(8,128)S(1)}, bf16[16,4096]{1,0:T(8,128)(2,1)S(1)}) custom-call(s32[8,16]{1,0:T(8,128)S(1)} %get-tuple-element.38.far_ref, bf16[12,256,80]{2,1,0:T(8,128)(2,1)S(1)} %get-tuple-element.40.far_src, bf16[12,32,256]{2,1,0:T(8,128)(2,1)S(1)} %get-tuple-element.41.far_w, bf16[16,80,256]{2,1,0:T(8,128)(2,1)S(1)} %get-tuple-element.42.far_tgt, ...), custom_call_target="tpu_custom_call" | custom-call | flops 4000000000 | bytes 1048576 | tf_op jit(solution)/shard_map/pallas_call | solution.py:21
  36.2 0.5 %collective-permute-start.9 = (bf16[16,4096]{1,0:T(8,128)(2,1)S(1)}, bf16[16,4096]{1,0:T(8,128)(2,1)S(1)}, u32[]{:S(2)}, u32[]{:S(2)}) collective-permute-start(bf16[16,4096]{1,0:T(8,128)(2,1)S(1)} %get-tuple-element.44), channel_id=1, source_target_pairs={{0,1},{1,0},{2,3},{3,2},{4,5},{5,4},{6,7},{7,6},{8,9},{9,8},{10,11... | collective-permute-start | bytes 393224 | tf_op jit(solution)/shard_map/ppermute | solution.py:419
  36.7 1.2 %shard_map.73.refs_0_.comp_ref = s32[1,8192]{1,0:T(1,128)S(1)} custom-call(s32[1,8192]{1,0:T(1,128)S(1)} %copy-done.3, s32[16,512]{1,0:T(8,128)S(1)} %copy-done.2), custom_call_target="tpu_custom_call" | custom-call | flops 1000000000 | bytes 1048576 | tf_op jit(solution)/shard_map/pallas_call | solution.py:21
  37.9 2.6 %collective-permute-done.7.refs_1_ = bf16[16,8192]{1,0:T(8,128)(2,1)S(1)} collective-permute-done((bf16[16,8192]{1,0:T(8,128)(2,1)S(1)}, bf16[16,8192]{1,0:T(8,128)(2,1)S(1)}, u32[]{:S(2)}, u32[]{:S(2)}) %collective-permute-start.7) | collective-permute-done | bytes 262176 | tf_op jit(solution)/shard_map/ppermute | solution.py:419
  40.6 0.6 %collective-permute-start.10 = (bf16[16,2048]{1,0:T(8,128)(2,1)S(1)}, bf16[16,2048]{1,0:T(8,128)(2,1)S(1)}, u32[]{:S(2)}, u32[]{:S(2)}) collective-permute-start(bf16[16,2048]{1,0:T(8,128)(2,1)S(1)} %get-tuple-element.45.refs_0_), channel_id=1, source_target_pairs={{0,2},{2,0},{1,3},{3,1},{4,6},{6,4},{5,7},{7,5},{8,10},{10,8},{9,1... | collective-permute-start | bytes 196616 | tf_op jit(solution)/shard_map/ppermute | solution.py:419
  41.2 1.4 %collective-permute-start.11 = (bf16[16,2048]{1,0:T(8,128)(2,1)S(1)}, bf16[16,2048]{1,0:T(8,128)(2,1)S(1)}, u32[]{:S(2)}, u32[]{:S(2)}) collective-permute-start(bf16[16,2048]{1,0:T(8,128)(2,1)S(1)} %get-tuple-element.46.refs_0_), channel_id=1, source_target_pairs={{0,2},{2,0},{1,3},{3,1},{4,6},{6,4},{5,7},{7,5},{8,10},{10,8},{9,1... | collective-permute-start | bytes 196616 | tf_op jit(solution)/shard_map/ppermute | solution.py:419
  42.6 2.4 %shard_map.78.start_ref = f32[512,256]{1,0:T(8,128)S(1)} custom-call(s32[1,8192]{1,0:T(1,128)S(1)} %copy-done.3, bf16[16,8192]{1,0:T(8,128)(2,1)S(1)} %add_convert_fusion.refs_0_.after_ref, bf16[16,8192]{1,0:T(8,128)(2,1)S(1)} %collective-permute-done.7.refs_1_), custom_call_target="tpu_custom_call" | custom-call | flops 3000000000 | bytes 1048576 | tf_op jit(solution)/shard_map/pallas_call | solution.py:21
  45.0 1.4 %shard_map.82.start_ref = f32[512,256]{1,0:T(8,128)S(1)} custom-call(s32[1,8192]{1,0:T(1,128)S(1)} %shard_map.73.refs_0_.comp_ref, bf16[16,256,256]{2,1,0:T(8,128)(2,1)S(1)} %copy-done.1, f32[512,256]{1,0:T(8,128)S(1)} %shard_map.78.start_ref, bf16[16,2048]{1,0:T(8,128)(2,1)S(1)} %get-tuple-element.45.refs_0_, ...), custom_call_target="tpu_custom_call" | custom-call | flops 2000000000 | bytes 1048576 | tf_op jit(solution)/shard_map/pallas_call | solution.py:21
  46.5 2.2 %shard_map.83 = f32[16,8192]{1,0:T(8,128)} custom-call(s32[1,8192]{1,0:T(1,128)S(1)} %shard_map.73.refs_0_.comp_ref, bf16[16,256,256]{2,1,0:T(8,128)(2,1)S(1)} %copy-done.1, f32[512,256]{1,0:T(8,128)S(1)} %shard_map.82.start_ref, bf16[16,2048]{1,0:T(8,128)(2,1)S(1)} %get-tuple-element.46.refs_0_, bf16[16,2048]{1,0:T(8,128)(2,1)S(1)} %collective-permute-done.11.refs_1_), custom_call_target="tpu_custom_call" | custom-call | flops 2000000000 | bytes 1048576 | tf_op jit(solution)/shard_map/pallas_call | solution.py:21
  (20 shorter events, 0.2 us)
Async XLA Ops:
  0.0 4.7 %collective-permute-start = (bf16[16,8192]{1,0:T(8,128)(2,1)}, bf16[16,8192]{1,0:T(8,128)(2,1)S(1)}, u32[]{:S(2)}, u32[]{:S(2)}) collective-permute-start(bf16[16,8192]{1,0:T(8,128)(2,1)} %bitcast.10), channel_id=1, source_target_pairs={{0,1},{1,0},{2,3},{3,2},{4,5},{5,4},{6,7},{7,6},{8,9},{9,8},{10,11... | collective-permute-start | bytes 786440 | tf_op jit(solution)/shard_map/ppermute | solution.py:419
  1.0 3.7 %collective-permute-start.1 = (s32[12,16]{1,0:T(8,128)S(1)}, s32[12,16]{1,0:T(8,128)S(1)}, u32[]{:S(2)}, u32[]{:S(2)}) collective-permute-start(s32[12,16]{1,0:T(8,128)S(1)} %get-tuple-element.26.refs_0_), channel_id=1, source_target_pairs={{0,2},{2,0},{1,3},{3,1},{4,6},{6,4},{5,7},{7,5},{8,10},{10,8},{9,1... | collective-permute-start | bytes 2312 | tf_op jit(solution)/shard_map/ppermute | solution.py:419
  2.6 10.3 %collective-permute-start.2 = (bf16[2,64,512]{2,1,0:T(8,128)(2,1)S(1)}, bf16[2,64,512]{2,1,0:T(8,128)(2,1)S(1)}, u32[]{:S(2)}, u32[]{:S(2)}) collective-permute-start(bf16[2,64,512]{2,1,0:T(8,128)(2,1)S(1)} %get-tuple-element.29), channel_id=1, source_target_pairs={{0,4},{4,8},{8,12},{12,0},{1,5},{5,9},{9,13},{13,1},{2,6},{6,10},{... | collective-permute-start | bytes 393224 | tf_op jit(solution)/shard_map/ppermute | solution.py:459
  4.2 8.8 %copy-start = (bf16[16,512,64]{1,2,0:T(8,128)(2,1)S(1)}, bf16[16,512,64]{1,2,0:T(8,128)(2,1)}, u32[]{:S(2)}) copy-start(bf16[16,512,64]{1,2,0:T(8,128)(2,1)} %param.7) | copy-start | bytes 3145732
  4.2 8.8 %copy-start.2 = (s32[16,512]{1,0:T(8,128)S(1)}, s32[16,512]{1,0:T(8,128)}, u32[]{:S(2)}) copy-start(s32[16,512]{1,0:T(8,128)} %skel_ref.5) | copy-start | bytes 98308
  4.2 8.7 %collective-permute-start.3 = (bf16[2,64,512]{2,1,0:T(8,128)(2,1)S(1)}, bf16[2,64,512]{2,1,0:T(8,128)(2,1)S(1)}, u32[]{:S(2)}, u32[]{:S(2)}) collective-permute-start(bf16[2,64,512]{2,1,0:T(8,128)(2,1)S(1)} %get-tuple-element.30), channel_id=1, source_target_pairs={{0,12},{4,0},{8,4},{12,8},{1,13},{5,1},{9,5},{13,9},{2,14},{6,2},{... | collective-permute-start | bytes 393224 | tf_op jit(solution)/shard_map/ppermute | solution.py:460
  8.2 17.6 %collective-permute-start.4 = (bf16[400,256]{1,0:T(8,128)(2,1)S(1)}, bf16[400,256]{1,0:T(8,128)(2,1)S(1)}, u32[]{:S(2)}, u32[]{:S(2)}) collective-permute-start(bf16[400,256]{1,0:T(8,128)(2,1)S(1)} %get-tuple-element.34), channel_id=1, source_target_pairs={{0,4},{4,8},{8,12},{12,0},{1,5},{5,9},{9,13},{13,1},{2,6},{6,10},{... | collective-permute-start | bytes 614408 | tf_op jit(solution)/shard_map/ppermute | solution.py:489
  9.9 16.4 %collective-permute-start.5 = (bf16[400,256]{1,0:T(8,128)(2,1)S(1)}, bf16[400,256]{1,0:T(8,128)(2,1)S(1)}, u32[]{:S(2)}, u32[]{:S(2)}) collective-permute-start(bf16[400,256]{1,0:T(8,128)(2,1)S(1)} %get-tuple-element.35), channel_id=1, source_target_pairs={{0,12},{4,0},{8,4},{12,8},{1,13},{5,1},{9,5},{13,9},{2,14},{6,2},{... | collective-permute-start | bytes 614408 | tf_op jit(solution)/shard_map/ppermute | solution.py:489
  10.5 20.0 %collective-permute-start.8 = (bf16[384,256]{1,0:T(8,128)(2,1)S(1)}, bf16[384,256]{1,0:T(8,128)(2,1)S(1)}, u32[]{:S(2)}, u32[]{:S(2)}) collective-permute-start(bf16[384,256]{1,0:T(8,128)(2,1)S(1)} %get-tuple-element.39), channel_id=1, source_target_pairs={{0,8},{4,12},{8,0},{12,4},{1,9},{5,13},{9,1},{13,5},{2,10},{6,14},... | collective-permute-start | bytes 589832 | tf_op jit(solution)/shard_map/ppermute | solution.py:489
  30.4 1.6 %collective-permute-start.6 = (bf16[16,8192]{1,0:T(8,128)(2,1)S(1)}, bf16[16,8192]{1,0:T(8,128)(2,1)S(1)}, u32[]{:S(2)}, u32[]{:S(2)}) collective-permute-start(bf16[16,8192]{1,0:T(8,128)(2,1)S(1)} %get-tuple-element.37), channel_id=1, source_target_pairs={{0,1},{1,0},{2,3},{3,2},{4,5},{5,4},{6,7},{7,6},{8,9},{9,8},{10,11... | collective-permute-start | bytes 786440 | tf_op jit(solution)/shard_map/ppermute | solution.py:419
  32.1 8.4 %collective-permute-start.7 = (bf16[16,8192]{1,0:T(8,128)(2,1)S(1)}, bf16[16,8192]{1,0:T(8,128)(2,1)S(1)}, u32[]{:S(2)}, u32[]{:S(2)}) collective-permute-start(bf16[16,8192]{1,0:T(8,128)(2,1)S(1)} %add_convert_fusion.refs_0_.after_ref), channel_id=1, source_target_pairs={{0,2},{2,0},{1,3},{3,1},{4,6},{6,4},{5,7},{7,5},{8,10},{10,8},{9,1... | collective-permute-start | bytes 786440 | tf_op jit(solution)/shard_map/ppermute | solution.py:419
  32.8 3.9 %copy-start.3 = (s32[1,8192]{1,0:T(1,128)S(1)}, s32[1,8192]{1,0:T(1,128)}, u32[]{:S(2)}) copy-start(s32[1,8192]{1,0:T(1,128)} %order_ref.5) | copy-start | bytes 98308
  36.2 1.7 %collective-permute-start.9 = (bf16[16,4096]{1,0:T(8,128)(2,1)S(1)}, bf16[16,4096]{1,0:T(8,128)(2,1)S(1)}, u32[]{:S(2)}, u32[]{:S(2)}) collective-permute-start(bf16[16,4096]{1,0:T(8,128)(2,1)S(1)} %get-tuple-element.44), channel_id=1, source_target_pairs={{0,1},{1,0},{2,3},{3,2},{4,5},{5,4},{6,7},{7,6},{8,9},{9,8},{10,11... | collective-permute-start | bytes 393224 | tf_op jit(solution)/shard_map/ppermute | solution.py:419
  40.6 4.5 %collective-permute-start.10 = (bf16[16,2048]{1,0:T(8,128)(2,1)S(1)}, bf16[16,2048]{1,0:T(8,128)(2,1)S(1)}, u32[]{:S(2)}, u32[]{:S(2)}) collective-permute-start(bf16[16,2048]{1,0:T(8,128)(2,1)S(1)} %get-tuple-element.45.refs_0_), channel_id=1, source_target_pairs={{0,2},{2,0},{1,3},{3,1},{4,6},{6,4},{5,7},{7,5},{8,10},{10,8},{9,1... | collective-permute-start | bytes 196616 | tf_op jit(solution)/shard_map/ppermute | solution.py:419
  41.2 3.8 %copy-start.1 = (bf16[16,256,256]{2,1,0:T(8,128)(2,1)S(1)}, bf16[16,256,256]{2,1,0:T(8,128)(2,1)}, u32[]{:S(2)}) copy-start(bf16[16,256,256]{2,1,0:T(8,128)(2,1)} %interp_ref.5) | copy-start | bytes 6291460
  41.2 5.3 %collective-permute-start.11 = (bf16[16,2048]{1,0:T(8,128)(2,1)S(1)}, bf16[16,2048]{1,0:T(8,128)(2,1)S(1)}, u32[]{:S(2)}, u32[]{:S(2)}) collective-permute-start(bf16[16,2048]{1,0:T(8,128)(2,1)S(1)} %get-tuple-element.46.refs_0_), channel_id=1, source_target_pairs={{0,2},{2,0},{1,3},{3,1},{4,6},{6,4},{5,7},{7,5},{8,10},{10,8},{9,1... | collective-permute-start | bytes 196616 | tf_op jit(solution)/shard_map/ppermute | solution.py:419
